TPU v7x, 32 devices: a whole 2x2x4 slice. The times are simulated.
32 devices in a mesh: tm: 16 (over z, y, core), batch: 2 (over x).
Axes of the slice: x: 2, y: 2, z: 4, core: 2. Of those that a mesh axis runs over, the one named last changes fastest.
Arguments:
- source_narrow: bfloat16 [3, 8, 2048, 256], P(None, 'batch', 'tm'), may hold values from -12 to 12
- source_wide: bfloat16 [2, 8, 2048, 384], P(None, 'batch', 'tm'), may hold values from -12 to 12
- lengths: int32 [8], P('batch'), may hold values from 512 to 2048, as said below
- cotangent: bfloat16 [8, 2048, 512], P('batch', 'tm'), may hold values from -6 to 6
- kernel_first: float32 [6528, 512], P('tm'), may hold values from -0.078125 to 0.078125
- kernel_rest: float32 [4, 8704, 512], P(None, 'tm'), may hold values from -0.0625 to 0.0625
- mixer_narrow: float32 [3, 256, 512], P(None, 'tm'), may hold values from -0.375 to 0.375
- mixer_wide: float32 [2, 384, 512], P(None, 'tm'), may hold values from -0.3125 to 0.3125
- norm_params: float32 [2, 10, 512], replicated, may hold values from -0.4 to 4, as said below
- moment_first: float32 [6528, 512], P('tm'), may hold values from -0.03125 to 0.03125
- square_first: float32 [6528, 512], P('tm'), may hold values from 2.2763695e-07 to 3.6421911e-06
- moment_rest: float32 [4, 8704, 512], P(None, 'tm'), may hold values from -0.03125 to 0.03125
- square_rest: float32 [4, 8704, 512], P(None, 'tm'), may hold values from 2.2763695e-07 to 3.6421911e-06
- moment_narrow: float32 [3, 256, 512], P(None, 'tm'), may hold values from -0.03125 to 0.03125
- square_narrow: float32 [3, 256, 512], P(None, 'tm'), may hold values from 2.2763695e-07 to 3.6421911e-06
- moment_wide: float32 [2, 384, 512], P(None, 'tm'), may hold values from -0.03125 to 0.03125
- square_wide: float32 [2, 384, 512], P(None, 'tm'), may hold values from 2.2763695e-07 to 3.6421911e-06
- moment_norm: float32 [2, 10, 512], replicated, may hold values from -0.0625 to 0.0625
- square_norm: float32 [2, 10, 512], replicated, may hold values from 9.105478e-08 to 3.6421912e-07
Outputs:
- mixed: bfloat16 [8, 2048, 512], P('batch', 'tm')
- grad_narrow: float32 [3, 8, 2048, 256], P(None, 'batch', 'tm')
- source_wide_gradient: float32 [2, 8, 2048, 384], P(None, 'batch', 'tm')
- grad_norm: float32 [], replicated
- new_first: float32 [6528, 512], P('tm')
- next_moment_first: float32 [6528, 512], P('tm')
- next_square_first: float32 [6528, 512], P('tm')
- new_rest: float32 [4, 8704, 512], P(None, 'tm')
- next_moment_rest: float32 [4, 8704, 512], P(None, 'tm')
- next_square_rest: float32 [4, 8704, 512], P(None, 'tm')
- new_narrow: float32 [3, 256, 512], P(None, 'tm')
- next_moment_narrow: float32 [3, 256, 512], P(None, 'tm')
- updated_square_mixer_narrow: float32 [3, 256, 512], P(None, 'tm')
- new_wide: float32 [2, 384, 512], P(None, 'tm')
- next_moment_wide: float32 [2, 384, 512], P(None, 'tm')
- next_square_wide: float32 [2, 384, 512], P(None, 'tm')
- new_norm: float32 [2, 10, 512], replicated
- next_moment_norm: float32 [2, 10, 512], replicated
- next_square_norm: float32 [2, 10, 512], replicated
Inputs may be any that keep to these rules, and one draw needn't show every extreme that they name: `lengths`: in each aligned group of 4 sequences, one sequence drawn from the seed has length 2048. `norm_params`: row 0 holds gains, row 1 biases.
All inputs are finite; a program needn't handle non-finite values.
Results may differ from a plain program's by a relative error of at most 0.02.
Values may be sent and summed in bfloat16 or wider, within the bound.
A program may use at most 384 MiB of HBM per device.

v0:
```python
import jax
import jax.numpy as jnp
from jax import lax
from jax.sharding import PartitionSpec as P

CO = 512
CW = 384
K = 17
STEP = 10


EPS = 1e-05
THRESHOLD = 100.0
BETA_ONE = 0.9
SECOND_DECAY = 0.999
ADAM_EPS = 1e-08
RATE_WEIGHT = 0.02
RATE_NORM = 0.4
DECAY = 0.01


def padded_2(shard, sides, width):
    for axis, dim in sides:
        devices, length = (lax.axis_size(axis), shard.shape[dim])
        up = [(i, (i + 1) % devices) for i in range(devices - 1)]
        down = [(j, i) for i, j in up]
        last = lax.slice_in_dim(shard, length - width, length, axis=dim)
        initial = lax.slice_in_dim(shard, 0, width, axis=dim)
        before = lax.ppermute(last, axis, up)
        after = lax.ppermute(initial, axis, down)
        shard = jnp.concatenate([before, shard, after], axis=dim)
    return shard


def adamw(param, grad, first, second, rate, decay):
    first_new = BETA_ONE * first + (1.0 - BETA_ONE) * grad
    second_new = SECOND_DECAY * second + (1.0 - SECOND_DECAY) * grad * grad
    fix_one = 1.0 - BETA_ONE**STEP
    fix_two = 1.0 - SECOND_DECAY**STEP
    update = first_new / fix_one / (jnp.sqrt(second_new / fix_two) + ADAM_EPS)
    return (param - rate * (update + decay * param), first_new, second_new)


def body(
    source_narrow,
    source_wide,
    lengths,
    cotangent,
    kernel_first,
    kernel_rest,
    mixer_narrow,
    mixer_wide,
    norm_params,
    moment_first,
    square_first,
    moment_rest,
    square_rest,
    moment_narrow,
    square_narrow,
    moment_wide,
    square_wide,
    moment_norm,
    square_norm,
):
    frames = source_wide.shape[2]
    half = K // 2
    places = lax.axis_index("tm") * frames + jnp.arange(frames, dtype=jnp.int32)
    valid = (places[None, :] < lengths[:, None]).astype(jnp.float32)[:, :, None]
    local_count = jnp.sum(valid)
    valid_low = valid.astype(jnp.bfloat16)
    narrow = source_narrow * valid_low[None]
    wide = source_wide * valid_low[None]
    full_first, full_rest, full_narrow, full_wide = (
        lax.all_gather(kernel_first.astype(jnp.bfloat16), "tm", axis=0, tiled=True),
        lax.all_gather(kernel_rest.astype(jnp.bfloat16), "tm", axis=1, tiled=True),
        lax.all_gather(mixer_narrow.astype(jnp.bfloat16), "tm", axis=1, tiled=True),
        lax.all_gather(mixer_wide.astype(jnp.bfloat16), "tm", axis=1, tiled=True),
    )
    kernels = [jnp.transpose(full_first.reshape(CW, K, CO), (1, 0, 2))] + [
        jnp.transpose(full_rest[layer].reshape(CO, K, CO), (1, 0, 2)) for layer in range(4)
    ]
    gains = norm_params[0]
    biases = norm_params[1]

    def batch_statistics(values, count):
        sums = tuple((jnp.sum(value * valid, axis=(0, 1)) for value in values))
        extra = (local_count,) if count is None else ()
        got = lax.psum(sums + extra, ("tm", "batch"))
        if count is None:
            count = got[-1]
        means = [total / count for total in got[: len(values)]]
        spreads = tuple(
            (
                jnp.sum(jnp.square((value - mean) * valid), axis=(0, 1))
                for value, mean in zip(values, means)
            )
        )
        second = lax.psum(spreads, ("tm", "batch"))
        variances = [total / count for total in second]
        scales = [lax.rsqrt(variance + EPS) for variance in variances]
        return (means, scales, count)

    signal = wide[1]
    kept = []
    count = None
    for index in range(5):
        padded = padded_2(signal, (("tm", 1),), half)
        field = jnp.zeros(signal.shape[:2] + (CO,), jnp.float32)
        for tap in range(K):
            field = field + jnp.einsum(
                "btc,cd->btd",
                padded[:, tap : tap + frames],
                kernels[index][tap],
                preferred_element_type=jnp.float32,
            )
        values = [field]
        indices = [index]
        if index == 4:
            for source in range(3):
                values.append(
                    jnp.einsum(
                        "btc,cd->btd",
                        narrow[source],
                        full_narrow[source],
                        preferred_element_type=jnp.float32,
                    )
                )
                indices.append(5 + source)
            for source in range(2):
                values.append(
                    jnp.einsum(
                        "btc,cd->btd",
                        wide[source],
                        full_wide[source],
                        preferred_element_type=jnp.float32,
                    )
                )
                indices.append(8 + source)
        means, scales, count = batch_statistics(values, count)
        normalized_values = [
            (value - mean) * scale for value, mean, scale in zip(values, means, scales)
        ]
        summed = jnp.zeros_like(field)
        for place in range(len(values)):
            summed = (
                summed + gains[indices[place]] * normalized_values[place] + biases[indices[place]]
            )
        kept.append((padded, normalized_values, scales, summed, indices))
        active = jax.nn.silu(summed) * valid
        signal = active.astype(jnp.bfloat16)
    grad_active = cotangent.astype(jnp.float32)
    kernel_grads = [None] * 5
    gain_grads = [None] * 10
    bias_grads = [None] * 10
    narrow_grads = []
    wide_grads = []
    narrow_inputs = []
    wide_inputs = []
    first_input = None
    for index in reversed(range(5)):
        padded, normalized_values, scales, summed, indices = kept[index]
        sigma = jax.nn.sigmoid(summed)
        gradient_total = grad_active * valid * sigma * (1.0 + summed * (1.0 - sigma))
        local_sums = (jnp.sum(gradient_total, axis=(0, 1)),) + tuple(
            (
                jnp.sum(gradient_total * standardized_input, axis=(0, 1))
                for standardized_input in normalized_values
            )
        )
        got = lax.psum(local_sums, ("tm", "batch"))
        bias_total = got[0]
        field_grads = []
        for place in range(len(normalized_values)):
            which = indices[place]
            gain = gains[which]
            gain_grads[which] = got[1 + place]
            bias_grads[which] = bias_total
            grad_field = scales[place] * (
                gain * gradient_total
                - valid * (gain * bias_total) / count
                - valid * normalized_values[place] * (gain * got[1 + place]) / count
            )
            field_grads.append(grad_field.astype(jnp.bfloat16))
        grad_conv = field_grads[0]
        tap_grads = [
            jnp.einsum(
                "btc,btd->cd",
                padded[:, tap : tap + frames],
                grad_conv,
                preferred_element_type=jnp.float32,
            )
            for tap in range(K)
        ]
        kernel_grads[index] = jnp.stack(tap_grads, axis=1).reshape(padded.shape[2] * K, CO)
        if index == 4:
            for source in range(3):
                branch = field_grads[1 + source]
                narrow_grads.append(
                    jnp.einsum(
                        "btc,btd->cd", narrow[source], branch, preferred_element_type=jnp.float32
                    )
                )
                narrow_inputs.append(
                    jnp.einsum(
                        "btd,cd->btc",
                        branch,
                        full_narrow[source],
                        preferred_element_type=jnp.float32,
                    )
                    * valid
                )
            for source in range(2):
                branch = field_grads[4 + source]
                wide_grads.append(
                    jnp.einsum(
                        "btc,btd->cd", wide[source], branch, preferred_element_type=jnp.float32
                    )
                )
                wide_inputs.append(
                    jnp.einsum(
                        "btd,cd->btc", branch, full_wide[source], preferred_element_type=jnp.float32
                    )
                    * valid
                )
        grad_padded = padded_2(grad_conv, (("tm", 1),), half)
        incoming = jnp.zeros(padded.shape[:1] + (frames, padded.shape[2]), jnp.float32)
        for tap in range(K):
            start = K - 1 - tap
            incoming = incoming + jnp.einsum(
                "btd,cd->btc",
                grad_padded[:, start : start + frames],
                kernels[index][tap],
                preferred_element_type=jnp.float32,
            )
        if index > 0:
            grad_active = incoming
        else:
            first_input = incoming
    grad_narrow = jnp.stack(narrow_inputs)
    source_wide_gradient = jnp.stack([wide_inputs[0], (first_input + wide_inputs[1]) * valid])
    shard_gradients = (
        kernel_grads[0],
        jnp.stack(kernel_grads[1:]),
        jnp.stack(narrow_grads),
        jnp.stack(wide_grads),
    )
    shards = (
        lax.psum_scatter(shard_gradients[0], "tm", scatter_dimension=0, tiled=True),
        lax.psum_scatter(shard_gradients[1], "tm", scatter_dimension=1, tiled=True),
        lax.psum_scatter(shard_gradients[2], "tm", scatter_dimension=1, tiled=True),
        lax.psum_scatter(shard_gradients[3], "tm", scatter_dimension=1, tiled=True),
    )
    norm_grad = jnp.stack([jnp.stack(gain_grads), jnp.stack(bias_grads)])
    params = (kernel_first, kernel_rest, mixer_narrow, mixer_wide)
    firsts = (moment_first, moment_rest, moment_narrow, moment_wide)
    seconds = (square_first, square_rest, square_narrow, square_wide)
    results = []
    shards = (
        lax.psum(shards[0].astype(jnp.bfloat16), "batch").astype(jnp.float32),
        lax.psum(shards[1].astype(jnp.bfloat16), "batch").astype(jnp.float32),
        lax.psum(shards[2].astype(jnp.bfloat16), "batch").astype(jnp.float32),
        lax.psum(shards[3].astype(jnp.bfloat16), "batch").astype(jnp.float32),
    )
    local_square = jnp.zeros((), jnp.float32)
    for shard in shards:
        local_square = local_square + jnp.sum(shard * shard)
    total = lax.psum(local_square, "tm") + jnp.sum(norm_grad * norm_grad)
    grad_norm = jnp.sqrt(total)
    clip = jnp.minimum(1.0, THRESHOLD / grad_norm)
    for slot in range(4):
        results.append(
            adamw(
                params[slot], clip * shards[slot], firsts[slot], seconds[slot], RATE_WEIGHT, DECAY
            )
        )
    results.append(adamw(norm_params, clip * norm_grad, moment_norm, square_norm, RATE_NORM, 0.0))
    return (
        signal,
        grad_narrow,
        source_wide_gradient,
        grad_norm,
        results[0][0],
        results[0][1],
        results[0][2],
        results[1][0],
        results[1][1],
        results[1][2],
        results[2][0],
        results[2][1],
        results[2][2],
        results[3][0],
        results[3][1],
        results[3][2],
        results[4][0],
        results[4][1],
        results[4][2],
    )


def solution(mesh):
    in_specs = (
        P(None, "batch", "tm", None),
        P(None, "batch", "tm", None),
        P("batch"),
        P("batch", "tm", None),
        P("tm", None),
        P(None, "tm", None),
        P(None, "tm", None),
        P(None, "tm", None),
        P(),
        P("tm", None),
        P("tm", None),
        P(None, "tm", None),
        P(None, "tm", None),
        P(None, "tm", None),
        P(None, "tm", None),
        P(None, "tm", None),
        P(None, "tm", None),
        P(),
        P(),
    )
    out_specs = (
        P("batch", "tm", None),
        P(None, "batch", "tm", None),
        P(None, "batch", "tm", None),
        P(),
        P("tm", None),
        P("tm", None),
        P("tm", None),
        P(None, "tm", None),
        P(None, "tm", None),
        P(None, "tm", None),
        P(None, "tm", None),
        P(None, "tm", None),
        P(None, "tm", None),
        P(None, "tm", None),
        P(None, "tm", None),
        P(None, "tm", None),
        P(),
        P(),
        P(),
    )
    return jax.shard_map(body, mesh=mesh, in_specs=in_specs, out_specs=out_specs, check_vma=False)
```

profile of v0, /device:TPU:0, one launch (start us, length us, event | category | flops | bytes accessed | tf_op | source)
XLA Modules:
  0.0 2420.1 jit_solution(11784137176322863391)
XLA Ops:
  114.5 40.7 %all-reduce.7 = (f32[512]{0:T(512)S(1)}, f32[]{:T(128)}) all-reduce(f32[512]{0:T(512)S(1)} %get-tuple-element.204, f32[]{:T(128)} %convert_reduce_fusion), channel_id=1, replica_groups=mesh['tm'=16,'batch'=2] {'tm','batch'}, use_global_device_ids=true, to_apply=%region_1.0 | all-reduce | flops 513 | bytes 4104 | tf_op jit(solution)/shard_map/psum | solution.py:88
  156.1 40.9 %psum.289 = f32[512]{0:T(512)S(1)} all-reduce(f32[512]{0:T(512)S(1)} %multiply_reduce_fusion.28), channel_id=1, replica_groups=mesh['tm'=16,'batch'=2] {'tm','batch'}, use_global_device_ids=true, to_apply=%region_5.0 | all-reduce | flops 512 | bytes 4096 | tf_op jit(solution)/shard_map/psum | solution.py:98
  201.4 69.0 %all-gather.5.cloned.1.call-done = bf16[4,8704,512]{2,1,0:T(8,128)(2,1)} async-done(((bf16[4,544,512]{2,1,0:T(8,128)(2,1)}), bf16[4,8704,512]{2,1,0:T(8,128)(2,1)}) %all-gather.5.cloned.1.call-update) | async-done | bytes 35651600 | tf_op jit(solution)/shard_map/all_gather | solution.py:75
  333.5 39.4 %psum.290 = f32[512]{0:T(512)S(1)} all-reduce(f32[512]{0:T(512)S(1)} %get-tuple-element.206), channel_id=1, replica_groups=mesh['tm'=16,'batch'=2] {'tm','batch'}, use_global_device_ids=true, to_apply=%region_7.8 | all-reduce | flops 512 | bytes 4096 | tf_op jit(solution)/shard_map/psum | solution.py:88
  373.8 41.8 %psum.291 = f32[512]{0:T(512)S(1)} all-reduce(f32[512]{0:T(512)S(1)} %multiply_reduce_fusion.26), channel_id=1, replica_groups=mesh['tm'=16,'batch'=2] {'tm','batch'}, use_global_device_ids=true, to_apply=%region_9.10 | all-reduce | flops 512 | bytes 4096 | tf_op jit(solution)/shard_map/psum | solution.py:98
  521.7 41.8 %psum.292 = f32[512]{0:T(512)S(1)} all-reduce(f32[512]{0:T(512)S(1)} %get-tuple-element.208), channel_id=1, replica_groups=mesh['tm'=16,'batch'=2] {'tm','batch'}, use_global_device_ids=true, to_apply=%region_11.12 | all-reduce | flops 512 | bytes 4096 | tf_op jit(solution)/shard_map/psum | solution.py:88
  564.4 42.1 %psum.293 = f32[512]{0:T(512)S(1)} all-reduce(f32[512]{0:T(512)S(1)} %multiply_reduce_fusion.24), channel_id=1, replica_groups=mesh['tm'=16,'batch'=2] {'tm','batch'}, use_global_device_ids=true, to_apply=%region_13.14 | all-reduce | flops 512 | bytes 4096 | tf_op jit(solution)/shard_map/psum | solution.py:98
  628.9 40.7 %psum.294 = f32[512]{0:T(512)S(1)} all-reduce(f32[512]{0:T(512)S(1)} %get-tuple-element.210), channel_id=1, replica_groups=mesh['tm'=16,'batch'=2] {'tm','batch'}, use_global_device_ids=true, to_apply=%region_15.16 | all-reduce | flops 512 | bytes 4096 | tf_op jit(solution)/shard_map/psum | solution.py:88
  670.5 40.7 %psum.295 = f32[512]{0:T(512)S(1)} all-reduce(f32[512]{0:T(512)S(1)} %multiply_reduce_fusion.22), channel_id=1, replica_groups=mesh['tm'=16,'batch'=2] {'tm','batch'}, use_global_device_ids=true, to_apply=%region_17.18 | all-reduce | flops 512 | bytes 4096 | tf_op jit(solution)/shard_map/psum | solution.py:98
  744.9 41.3 %psum.296 = f32[512]{0:T(512)S(1)} all-reduce(f32[512]{0:T(512)S(1)} %get-tuple-element.212), channel_id=1, replica_groups=mesh['tm'=16,'batch'=2] {'tm','batch'}, use_global_device_ids=true, to_apply=%region_19.20 | all-reduce | flops 512 | bytes 4096 | tf_op jit(solution)/shard_map/psum | solution.py:88
  790.1 40.7 %all-reduce.6 = (f32[512]{0:T(512)S(1)}, f32[512]{0:T(512)S(1)}, f32[512]{0:T(512)S(1)}, f32[512]{0:T(512)S(1)}, f32[512]{0:T(512)S(1)}) all-reduce(f32[512]{0:T(512)S(1)} %get-tuple-element.72, f32[512]{0:T(512)S(1)} %get-tuple-element.73, f32[512]{0:T(512)S(1)} %get-tuple-element.74, ...), channel_id=1, replica_groups=mesh['tm'=16,'batch'=2] {'tm','batch'}, use_global_device_ids=true, to_apply=%region_23.24 | all-reduce | flops 2560 | bytes 20480 | tf_op jit(solution)/shard_map/psum | solution.py:88
  836.5 40.0 %all-reduce.5 = (f32[512]{0:T(512)S(1)}, f32[512]{0:T(512)S(1)}, f32[512]{0:T(512)S(1)}, f32[512]{0:T(512)S(1)}, f32[512]{0:T(512)S(1)}, /*index=5*/f32[512]{0:T(512)S(1)}) all-reduce(f32[512]{0:T(512)S(1)} %get-tuple-element.81, f32[512]{0:T(512)S(1)} %get-tuple-element.80, ...), channel_id=1, replica_groups=mesh['tm'=16,'batch'=2] {'tm','batch'}, use_global_device_ids=true, to_apply=%region_41.42 | all-reduce | flops 3072 | bytes 24576 | tf_op jit(solution)/shard_map/psum | solution.py:98
  885.3 40.7 %all-reduce.4 = (f32[512]{0:T(512)S(1)}, f32[512]{0:T(512)S(1)}) all-reduce(f32[512]{0:T(512)S(1)} %get-tuple-element.129, f32[512]{0:T(512)S(1)} %get-tuple-element.59), channel_id=1, replica_groups=mesh['tm'=16,'batch'=2] {'tm','batch'}, use_global_device_ids=true, to_apply=%region_43.44 | all-reduce | flops 1024 | bytes 8192 | tf_op jit(solution)/shard_map/psum | solution.py:170
  950.6 43.2 %all-reduce.3 = (f32[512]{0:T(512)S(1)}, f32[512]{0:T(512)S(1)}) all-reduce(f32[512]{0:T(512)S(1)} %get-tuple-element.70, f32[512]{0:T(512)S(1)} %get-tuple-element.69), channel_id=1, replica_groups=mesh['tm'=16,'batch'=2] {'tm','batch'}, use_global_device_ids=true, to_apply=%region_57.58 | all-reduce | flops 1024 | bytes 8192 | tf_op jit(solution)/shard_map/psum | solution.py:170
  1018.6 42.8 %all-reduce.2 = (f32[512]{0:T(512)S(1)}, f32[512]{0:T(512)S(1)}) all-reduce(f32[512]{0:T(512)S(1)} %get-tuple-element.68, f32[512]{0:T(512)S(1)} %get-tuple-element.67), channel_id=1, replica_groups=mesh['tm'=16,'batch'=2] {'tm','batch'}, use_global_device_ids=true, to_apply=%region_61.62 | all-reduce | flops 1024 | bytes 8192 | tf_op jit(solution)/shard_map/psum | solution.py:170
  1086.2 43.9 %all-reduce.1 = (f32[512]{0:T(512)S(1)}, f32[512]{0:T(512)S(1)}) all-reduce(f32[512]{0:T(512)S(1)} %get-tuple-element.66, f32[512]{0:T(512)S(1)} %get-tuple-element.65), channel_id=1, replica_groups=mesh['tm'=16,'batch'=2] {'tm','batch'}, use_global_device_ids=true, to_apply=%region_65.66 | all-reduce | flops 1024 | bytes 8192 | tf_op jit(solution)/shard_map/psum | solution.py:170
  1155.2 43.1 %all-reduce = (f32[512]{0:T(512)S(1)}, f32[512]{0:T(512)S(1)}, f32[512]{0:T(512)S(1)}, f32[512]{0:T(512)S(1)}, f32[512]{0:T(512)S(1)}, /*index=5*/f32[512]{0:T(512)S(1)}, f32[512]{0:T(512)S(1)}) all-reduce(f32[512]{0:T(512)S(1)} %get-tuple-element.60, ...), channel_id=1, replica_groups=mesh['tm'=16,'batch'=2] {'tm','batch'}, use_global_device_ids=true, to_apply=%region_49.50 | all-reduce | flops 3584 | bytes 28672 | tf_op jit(solution)/shard_map/psum | solution.py:170
  1347.1 33.7 %copy.311 = f32[512,17,512]{2,1,0:T(8,128)} copy(f32[512,17,512]{2,0,1:T(8,128)S(1)} %fusion.21) | data formatting | bytes 35651584 | tf_op jit(solution)/shard_map/stack | solution.py:194
  1409.4 33.5 %copy.293 = f32[512,17,512]{2,1,0:T(8,128)} copy(f32[512,17,512]{2,0,1:T(8,128)S(1)} %fusion.38) | data formatting | bytes 35651584 | tf_op jit(solution)/shard_map/stack | solution.py:194
  1471.6 33.5 %copy.275 = f32[512,17,512]{2,1,0:T(8,128)} copy(f32[512,17,512]{2,0,1:T(8,128)S(1)} %fusion.55) | data formatting | bytes 35651584 | tf_op jit(solution)/shard_map/stack | solution.py:194
  1525.5 47.1 %pad_maximum_fusion = f32[4,8704,512]{2,1,0:T(8,128)} fusion(f32[1,8704,512]{2,1,0:T(8,128)} %stack_reshape.15, f32[1,8704,512]{2,1,0:T(8,128)} %stack_reshape.14, f32[1,8704,512]{2,1,0:T(8,128)} %stack_reshape.13, f32[1,8704,512]{2,1,0:T(8,128)} %stack_reshape.12), kind=kLoop, calls=%fused_computation | loop fusion | flops 53477376 | bytes 142606336 | tf_op jit(solution)/shard_map/stack | solution.py:243
  1610.4 634.3 %reduce-scatter.7.cloned.1.call-done = f32[4,544,512]{2,1,0:T(8,128)} async-done(((f32[4,8704,512]{2,1,0:T(8,128)}), f32[4,544,512]{2,1,0:T(8,128)}) %reduce-scatter.7.cloned.1.call-update) | async-done | bytes 4456464 | tf_op jit(solution)/shard_map/reduce_scatter | solution.py:249
  2270.9 75.9 %all-reduce.15.cloned.1.call-done = (bf16[408,512]{1,0:T(8,128)(2,1)}, bf16[4,544,512]{2,1,0:T(8,128)(2,1)}) async-done(((bf16[408,512]{1,0:T(8,128)(2,1)}, bf16[4,544,512]{2,1,0:T(8,128)(2,1)}), (bf16[408,512]{1,0:T(8,128)(2,1)}, bf16[4,544,512]{2,1,0:T(8,128)(2,1)})) %all-reduce.15.cloned.1.call-update) | async-done | bytes 2646032 | tf_op jit(solution)/shard_map/psum | solution.py:259
  2357.4 33.7 %psum.327 = f32[]{:T(128)} all-reduce(f32[]{:T(128)S(6)} %add.1071), channel_id=1, replica_groups=mesh['tm'=16,'batch'=2] {'tm'}, use_global_device_ids=true, to_apply=%region_84.85 | all-reduce | flops 1 | bytes 8 | tf_op jit(solution)/shard_map/psum | solution.py:267
  (770 shorter events, 772.3 us)
Async XLA Ops:
  7.3 81.6 %all-gather.3.cloned.1.call-start = ((), (), s32[]{:S(2)}) async-start(), calls=%async_computation.4 | async-start | bytes 7102464 | tf_op jit(solution)/shard_map/all_gather | solution.py:74
  9.4 261.0 %all-gather.5.cloned.1.call-start = ((), (), s32[]{:S(2)}) async-start(), calls=%async_computation.5 | async-start | bytes 37879808 | tf_op jit(solution)/shard_map/all_gather | solution.py:75
  13.4 1589.0 %reduce-scatter.9.cloned.1.call-start = ((), (), s32[]{:S(2)}) async-start(), calls=%async_computation.8 | async-start | bytes 1671168 | tf_op jit(solution)/shard_map/reduce_scatter | solution.py:250
  13.8 95.5 %collective-permute-start = (bf16[4,8,384]{2,1,0:T(8,128)(2,1)S(1)}, bf16[4,8,384]{2,1,0:T(8,128)(2,1)S(1)}, u32[]{:S(2)}, u32[]{:S(2)}) collective-permute-start(bf16[4,8,384]{2,1,0:T(8,128)(2,1)S(1)} %get-tuple-element.158), channel_id=1, source_target_pairs={{0,2},{2,4},{4,6},{6,8},{8,10},{10,12},{12,14},{14,16},{16,18},{18... | collective-permute-start | bytes 73736 | tf_op jit(solution)/shard_map/ppermute | solution.py:29
  16.1 90.0 %collective-permute-start.1 = (bf16[4,8,384]{2,1,0:T(8,128)(2,1)S(1)}, bf16[4,8,384]{2,1,0:T(8,128)(2,1)S(1)}, u32[]{:S(2)}, u32[]{:S(2)}) collective-permute-start(bf16[4,8,384]{2,1,0:T(8,128)(2,1)S(1)} %get-tuple-element.159), channel_id=1, source_target_pairs={{2,0},{4,2},{6,4},{8,6},{10,8},{12,10},{14,12},{16,14},{18,16},{20... | collective-permute-start | bytes 73736 | tf_op jit(solution)/shard_map/ppermute | solution.py:30
  198.1 130.6 %collective-permute-start.2 = (bf16[4,8,512]{2,1,0:T(8,128)(2,1)S(1)}, bf16[4,8,512]{2,1,0:T(8,128)(2,1)S(1)}, u32[]{:S(2)}, u32[]{:S(2)}) collective-permute-start(bf16[4,8,512]{2,1,0:T(8,128)(2,1)S(1)} %get-tuple-element.156), channel_id=1, source_target_pairs={{0,2},{2,4},{4,6},{6,8},{8,10},{10,12},{12,14},{14,16},{16,18},{18... | collective-permute-start | bytes 98312 | tf_op jit(solution)/shard_map/ppermute | solution.py:29
  199.9 122.1 %collective-permute-start.3 = (bf16[4,8,512]{2,1,0:T(8,128)(2,1)S(1)}, bf16[4,8,512]{2,1,0:T(8,128)(2,1)S(1)}, u32[]{:S(2)}, u32[]{:S(2)}) collective-permute-start(bf16[4,8,512]{2,1,0:T(8,128)(2,1)S(1)} %get-tuple-element.157), channel_id=1, source_target_pairs={{2,0},{4,2},{6,4},{8,6},{10,8},{12,10},{14,12},{16,14},{18,16},{20... | collective-permute-start | bytes 98312 | tf_op jit(solution)/shard_map/ppermute | solution.py:30
  416.6 90.9 %collective-permute-start.4 = (bf16[4,8,512]{2,1,0:T(8,128)(2,1)S(1)}, bf16[4,8,512]{2,1,0:T(8,128)(2,1)S(1)}, u32[]{:S(2)}, u32[]{:S(2)}) collective-permute-start(bf16[4,8,512]{2,1,0:T(8,128)(2,1)S(1)} %get-tuple-element.154), channel_id=1, source_target_pairs={{0,2},{2,4},{4,6},{6,8},{8,10},{10,12},{12,14},{14,16},{16,18},{18... | collective-permute-start | bytes 98312 | tf_op jit(solution)/shard_map/ppermute | solution.py:29
  417.9 79.1 %collective-permute-start.5 = (bf16[4,8,512]{2,1,0:T(8,128)(2,1)S(1)}, bf16[4,8,512]{2,1,0:T(8,128)(2,1)S(1)}, u32[]{:S(2)}, u32[]{:S(2)}) collective-permute-start(bf16[4,8,512]{2,1,0:T(8,128)(2,1)S(1)} %get-tuple-element.155), channel_id=1, source_target_pairs={{2,0},{4,2},{6,4},{8,6},{10,8},{12,10},{14,12},{16,14},{18,16},{20... | collective-permute-start | bytes 98312 | tf_op jit(solution)/shard_map/ppermute | solution.py:30
  607.5 16.5 collective-permute-start.6
  608.8 5.6 collective-permute-start.7
  712.2 17.3 collective-permute-start.8
  713.5 5.6 collective-permute-start.9
  931.8 12.2 collective-permute-start.10
  999.6 12.4 collective-permute-start.12
  1067.2 12.4 collective-permute-start.14
  1135.9 12.6 collective-permute-start.16
  1212.7 391.3 %reduce-scatter.11.cloned.1.call-start = ((), (), s32[]{:S(2)}) async-start(), calls=%async_computation.9 | async-start | bytes 1671168 | tf_op jit(solution)/shard_map/reduce_scatter | solution.py:251
  1229.3 378.9 %reduce-scatter.5.cloned.1.call-start = ((), (), s32[]{:S(2)}) async-start(), calls=%async_computation.6 | async-start | bytes 14204928 | tf_op jit(solution)/shard_map/reduce_scatter | solution.py:248
  1277.0 967.7 %reduce-scatter.7.cloned.1.call-start = ((), (), s32[]{:S(2)}) async-start(), calls=%async_computation.7 | async-start | bytes 75759616 | tf_op jit(solution)/shard_map/reduce_scatter | solution.py:249
  1572.9 695.2 %all-reduce.13.cloned.1.call-start = ((), (), s32[]{:S(2)}) async-start(), calls=%async_computation.10 | async-start | bytes 196608 | tf_op jit(solution)/shard_map/psum | solution.py:261
  1573.7 675.0 %collective-permute-start.18 = (bf16[4,8,512]{2,1,0:T(8,128)(2,1)S(1)}, bf16[4,8,512]{2,1,0:T(8,128)(2,1)S(1)}, u32[]{:S(2)}, u32[]{:S(2)}) collective-permute-start(bf16[4,8,512]{2,1,0:T(8,128)(2,1)S(1)} %get-tuple-element.140), channel_id=1, source_target_pairs={{2,0},{4,2},{6,4},{8,6},{10,8},{12,10},{14,12},{16,14},{18,16},{20... | collective-permute-start | bytes 98312 | tf_op jit(solution)/shard_map/ppermute | solution.py:30
  1575.0 12.9 collective-permute-start.19
  1605.5 741.3 %all-reduce.15.cloned.1.call-start = ((), (), s32[]{:S(2)}) async-start(), calls=%async_computation.11 | async-start | bytes 5292032 | tf_op jit(solution)/shard_map/psum | solution.py:259
  (168 other events, 8204.4 us)
Sparse Core Ops, SparseCore 0:
  10.9 77.8 all-gather.2
  91.0 179.3 all-gather.4
  1212.7 59.6 reduce-scatter.8
  1277.0 58.4 reduce-scatter.10
  1339.5 139.1 reduce-scatter.4
  1572.8 671.8 reduce-scatter.6
  2247.7 20.3 all-reduce.12
  2271.7 75.0 all-reduce.14
where the time goes:
time: 2440 us; the launch traced here: 2420 us
  waiting for transfers between devices  800 us (33%)
  blocking collectives  751 us (31%)
  local copies, waits for them, and re-layouts  393 us (16%)
  matrix products  281 us (12%)
  other arithmetic  141 us (6%)
  starting transfers between devices  31.4 us (1%)
    reduce_scatter x1, waiting for transfers between devices, body(): lax.psum_scatter(shard_gradients[1], 'tm', scatter_dimension=1, tiled=True)  634 us
    psum x6, blocking collectives, batch_statistics(): got = lax.psum(sums + extra, ('tm', 'batch'))  245 us
    psum x5, blocking collectives, body(): got = lax.psum(local_sums, ('tm', 'batch'))  214 us
    psum x5, blocking collectives, batch_statistics(): second = lax.psum(spreads, ('tm', 'batch'))  205 us
    another operation x5, local copies, waits for them, and re-layouts, body(): jnp.stack(tap_grads, axis=1).reshape(padded.shape[2] * K, CO)  145 us
    dot_general x85, matrix products, body(): jnp.einsum('btd,cd->btc', grad_padded[:, start:start + frames], kernels[i...  108 us
    another operation x8, local copies, waits for them, and re-layouts, body(): full_rest[layer].reshape(CO, K, CO)  102 us
    dot_general x85, matrix products, body(): jnp.einsum('btc,cd->btd', padded[:, tap:tap + frames], kernels[index][tap...  89.8 us
  transfers between devices with their start and end apart: 28, of which 7 were waited for; matrix products, arithmetic and copies ran while one was open for 28% of the time, Pallas kernels for 0%

commit v1 on v0

--- a/solution.py
+++ b/solution.py
@@ -1,6 +1,9 @@
+import numpy as np
 import jax
 import jax.numpy as jnp
 from jax import lax
+from jax.experimental import pallas as pl
+from jax.experimental.pallas import tpu as pltpu
 from jax.sharding import PartitionSpec as P
 
 CO = 512
@@ -297,6 +300,1641 @@
     )
 
 
+BF = jnp.bfloat16
+F32 = jnp.float32
+MESH = pl.DeviceIdType.MESH
+ROWS = 1024
+HALO = 64
+HALF = 256
+GROUPS = 34
+
+
+def wait_on(ref, sem):
+    pltpu.make_async_copy(ref, ref, sem).wait()
+
+
+def remote(src, dst, send, recv, device):
+    pltpu.make_async_remote_copy(
+        src_ref=src,
+        dst_ref=dst,
+        send_sem=send,
+        recv_sem=recv,
+        device_id=device,
+        device_id_type=MESH,
+    ).start()
+
+
+def position():
+    x = lax.axis_index("batch")
+    t = lax.axis_index("tm")
+    return x, t, lax.div(t, 4), lax.rem(lax.div(t, 2), 2), lax.rem(t, 2)
+
+
+def greet(x, t):
+    barrier = pltpu.get_barrier_semaphore()
+
+    def one(d, _):
+        pl.semaphore_signal(
+            barrier, inc=1, device_id=(lax.rem(t + d, 16), x), device_id_type=MESH
+        )
+        return 0
+
+    lax.fori_loop(1, 16, one, 0)
+    for d in (0, 1, 15):
+        pl.semaphore_signal(
+            barrier, inc=1, device_id=(lax.rem(t + d, 16), 1 - x), device_id_type=MESH
+        )
+    pl.semaphore_wait(barrier, 18)
+
+
+def frame_mask(block, t, lens):
+    frames = lax.broadcasted_iota(jnp.int32, (16, 8, HALF), 0) + (block * 16 + t * 128)
+    return (frames.astype(F32) < lens[None]).astype(F32)
+
+
+def share(box, at, t, x, send, recv):
+    def one(d, _):
+        remote(box.at[at, t], box.at[at, t], send, recv, (lax.rem(t + d, 16), x))
+        return 0
+
+    lax.fori_loop(1, 16, one, 0)
+
+
+def forward_kernel(
+    lens_in,
+    norm,
+    perm,
+    src_n,
+    src_w,
+    cot,
+    kf,
+    kr,
+    mn,
+    mw,
+    w_out,
+    wmn_out,
+    wmw_out,
+    h_out,
+    xh_out,
+    y_out,
+    nar_out,
+    wid_out,
+    cot_out,
+    rs_out,
+    len_out,
+    W,
+    G,
+    wmn,
+    wmw,
+    hA,
+    hB,
+    z,
+    zb,
+    xhb,
+    y5,
+    stg,
+    pf,
+    pmn,
+    pmw,
+    raww,
+    rawn,
+    rawc,
+    nar,
+    wid,
+    cotv,
+    st,
+    nv,
+    lenr,
+    lens,
+    load_s,
+    ag_s,
+    rz,
+    ry,
+    rc,
+    m_s,
+    m_r,
+    x_s,
+    x_r,
+    xr_s,
+    xr_r,
+    halo_s,
+    halo_r,
+    st_s,
+    st_r,
+    out_s,
+):
+    x, t, zi, yi, ci = position()
+    cols = pl.ds(pl.multiple_of(x * HALF, HALF), HALF)
+    partner = (t, 1 - x)
+    sibling = (t + 1 - 2 * ci, x)
+    across = (zi * 4 + (1 - yi) * 2 + ci, x)
+
+    lanes = [pl.ds(pl.multiple_of(x * HALF + 128 * b, 128), 128) for b in range(2)]
+    loads = [(kf.at[:, lanes[b]], pf.at[0, b, pl.ds(0, 408)]) for b in range(2)]
+    loads += [(kr.at[i, :, lanes[b]], pf.at[1 + i, b]) for i in range(4) for b in range(2)]
+    loads += [
+        (mn.at[:, :, cols], pmn),
+        (mw.at[:, :, cols], pmw),
+        (src_w, raww.at[x]),
+        (src_n, rawn.at[x]),
+        (cot.at[:, :, cols], rawc.at[x]),
+    ]
+    copies = [pltpu.make_async_copy(a, b, load_s.at[i]) for i, (a, b) in enumerate(loads)]
+    for copy in copies:
+        copy.start()
+    hA[:, :, pl.ds(1152, 16), :] = jnp.zeros((5, 2, 16, HALF), BF)
+
+    @pl.when(t == 0)
+    def _():
+        hA[:, :, pl.ds(0, HALO), :] = jnp.zeros((5, 2, HALO, HALF), BF)
+
+    @pl.when(t == 15)
+    def _():
+        hA[:, :, pl.ds(1088, HALO), :] = jnp.zeros((5, 2, HALO, HALF), BF)
+
+    lenr[0] = lens_in[...]
+    greet(x, t)
+
+    other = pl.ds(pl.multiple_of((1 - x) * HALF, HALF), HALF)
+    remote(lenr.at[0], lenr.at[1], xr_s.at[0], xr_r.at[0], partner)
+    remote(src_w.at[1], raww.at[x, 1], xr_s.at[1], xr_r.at[1], partner)
+
+    def prep(layer, count):
+        for k in range(17):
+            for b in range(2):
+                v = pf[layer, b, pl.ds(k, count, stride=17), :]
+                if count < 32:
+                    v = jnp.concatenate([v, jnp.zeros((32 - count, 128), F32)], axis=0)
+                W[17 * layer + k, t, :, pl.ds(128 * b, 128)] = v.astype(BF)
+
+    def chunk(g, slot):
+        return W.at[
+            pl.ds(5 * lax.div(g, 2), 5), slot, pl.ds(pl.multiple_of(16 * lax.rem(g, 2), 16), 16)
+        ]
+
+    def amount(g, n):
+        return W.at[
+            pl.ds(5 * lax.div(g, 2), 5),
+            pl.ds(0, n),
+            pl.ds(pl.multiple_of(16 * lax.rem(g, 2), 16), 16),
+        ]
+
+    def along(dz):
+        return lax.rem(zi + dz, 4) * 4 + yi * 2 + ci
+
+    def own_sends(block, send, into_z, into_y, into_c):
+        mine = block(t)
+        for dz in (1, 2, 3):
+            remote(mine, mine, send, into_z, (along(dz), x))
+        remote(mine, mine, send, into_y, across)
+        remote(mine, mine, send, into_c, sibling)
+
+    def pass_z(block, send, into_y, into_c):
+        for dz in (1, 2, 3):
+            got = block(along(dz))
+            remote(got, got, send, into_y, across)
+            remote(got, got, send, into_c, sibling)
+
+    def pass_y(block, send, into_c):
+        for zz in range(4):
+            got = block(zz * 4 + (1 - yi) * 2 + ci)
+            remote(got, got, send, into_c, sibling)
+
+    def service(g):
+        @pl.when(g < GROUPS)
+        def _():
+            own_sends(lambda s: chunk(g, s), ag_s.at[g], rz.at[g], ry.at[g], rc.at[g])
+
+        @pl.when((g >= 1) & (g <= GROUPS))
+        def _():
+            h = g - 1
+            wait_on(amount(h, 3), rz.at[h])
+            pass_z(lambda s: chunk(h, s), ag_s.at[h], ry.at[h], rc.at[h])
+
+        @pl.when((g >= 2) & (g <= GROUPS + 1))
+        def _():
+            h = g - 2
+            wait_on(amount(h, 4), ry.at[h])
+            pass_y(lambda s: chunk(h, s), ag_s.at[h], rc.at[h])
+
+        @pl.when((g >= 3) & (g <= GROUPS + 2))
+        def _():
+            h = g - 3
+            wait_on(amount(h, 8), rc.at[h])
+
+        mixer = lambda s: G.at[s]
+
+        @pl.when(g == 8)
+        def _():
+            own_sends(mixer, m_s, m_r.at[0], m_r.at[1], m_r.at[2])
+
+        @pl.when(g == 9)
+        def _():
+            wait_on(G.at[pl.ds(0, 3)], m_r.at[0])
+            pass_z(mixer, m_s, m_r.at[1], m_r.at[2])
+
+        @pl.when(g == 10)
+        def _():
+            wait_on(G.at[pl.ds(0, 4)], m_r.at[1])
+            pass_y(mixer, m_s, m_r.at[2])
+
+        @pl.when(g == 11)
+        def _():
+            wait_on(G.at[pl.ds(0, 8)], m_r.at[2])
+            for j in range(3):
+                for s in range(16):
+                    wmn[j, pl.ds(16 * s, 16), :] = G[s, pl.ds(16 * j, 16), :]
+            for j in range(2):
+                for s in range(16):
+                    wmw[j, pl.ds(32 * s, 32), :] = G[s, pl.ds(48 + 32 * j, 32), :]
+
+    def serve(first, last):
+        def one(g, _):
+            service(g)
+            return 0
+
+        lax.fori_loop(first, last, one, 0)
+
+    for copy in copies[:2]:
+        copy.wait()
+    prep(0, 24)
+    service(jnp.int32(0))
+    for copy in copies[2:12]:
+        copy.wait()
+    prep(1, 32)
+    for layer in (2, 3, 4):
+        prep(layer, 32)
+    for j in range(3):
+        G[t, pl.ds(16 * j, 16), :] = pmn[j].astype(BF)
+    for j in range(2):
+        G[t, pl.ds(48 + 32 * j, 32), :] = jnp.concatenate(
+            [pmw[j], jnp.zeros((8, HALF), F32)], axis=0
+        ).astype(BF)
+    serve(1, 3)
+
+    wait_on(lenr.at[1], xr_r.at[0])
+    lens[...] = lenr[0] + lenr[1]
+    len_out[...] = lens[...]
+    for s in range(16):
+        nv[s] = jnp.broadcast_to(
+            jnp.sum(jnp.clip(lens[...] - 128.0 * s, 0.0, 128.0), axis=0, keepdims=True), (8, HALF)
+        )
+
+    def spread_wide(j):
+        for s in range(8):
+            v = jnp.dot(raww[s // 4, j, s % 4], perm[...], preferred_element_type=F32)
+            for b in range(4):
+                stg[b, pl.ds(s, 128, stride=8), :] = v[:, 128 * b : 128 * b + 128]
+
+    def spread_half(v, s):
+        for b in range(2):
+            stg[b, pl.ds(s, 128, stride=8), :] = v[:, 128 * b : 128 * b + 128].astype(F32)
+
+    def masked_block(b, h):
+        rows = pl.ds(pl.multiple_of(b * 128, 128), 128)
+        v = jnp.concatenate([stg[2 * h, rows, :], stg[2 * h + 1, rows, :]], axis=1)
+        v = v.reshape(16, 8, HALF)
+        return (v * frame_mask(b, t, lens[...])).reshape(128, HALF).astype(BF)
+
+    copies[12].wait()
+    wait_on(raww.at[0, 1], xr_r.at[1])
+    spread_wide(1)
+
+    def first_block(b, _):
+        for h in range(2):
+            hA[0, h, pl.ds(pl.multiple_of(HALO + b * 128, 64), 128), :] = masked_block(b, h)
+        return 0
+
+    lax.fori_loop(0, 8, first_block, 0)
+
+    def halo_send(layer, half, to, side):
+        a, b = ((HALO, 1088), (1024, 0))[side]
+        remote(
+            hA.at[layer, half, pl.ds(a, HALO)],
+            hA.at[layer, half, pl.ds(b, HALO)],
+            halo_s.at[layer, side, half if to is None else to],
+            halo_r.at[layer, side, half],
+            (t - 1 + 2 * side, x if to is None else jnp.where(to == 0, x, 1 - x)),
+        )
+
+    def halo_wait(layer, send):
+        @pl.when(t > 0)
+        def _():
+            for h in range(2):
+                wait_on(hA.at[layer, h, pl.ds(0, HALO)], (halo_s if send else halo_r).at[layer, 0 if send else 1, h])
+
+        @pl.when(t < 15)
+        def _():
+            for h in range(2):
+                wait_on(hA.at[layer, h, pl.ds(0, HALO)], (halo_s if send else halo_r).at[layer, 1 if send else 0, h])
+
+    @pl.when(t > 0)
+    def _():
+        for h in range(2):
+            halo_send(0, h, None, 0)
+
+    @pl.when(t < 15)
+    def _():
+        for h in range(2):
+            halo_send(0, h, None, 1)
+
+    remote(src_n, rawn.at[x], xr_s.at[2], xr_r.at[2], partner)
+    remote(src_w.at[0], raww.at[x, 0], xr_s.at[3], xr_r.at[3], partner)
+    serve(3, 11)
+
+    def shift_copy(layer):
+        def one(b, _):
+            for h in range(2):
+                v = hA[layer, h, pl.ds(pl.multiple_of(b * 128, 128), 144), :].astype(F32)
+                hB[h, pl.ds(pl.multiple_of(b * 128, 128), 128), :] = v[8:136].astype(BF)
+            return 0
+
+        lax.fori_loop(0, 9, one, 0)
+
+    halo_wait(0, False)
+    shift_copy(0)
+
+    def rows_of(b):
+        return pl.ds(pl.multiple_of(b * 128, 128), 128)
+
+    def local_stats(ref):
+        def total(b, acc):
+            v = ref[rows_of(b), :].reshape(16, 8, HALF) * frame_mask(b, t, lens[...])
+            return acc + jnp.sum(v, axis=0)
+
+        s = jnp.sum(
+            lax.fori_loop(0, 8, total, jnp.zeros((8, HALF), F32)), axis=0, keepdims=True
+        )
+        mean = s / jnp.maximum(nv[t, pl.ds(0, 1), :], 1.0)
+
+        def spread(b, acc):
+            v = (ref[rows_of(b), :].reshape(16, 8, HALF) - mean[None]) * frame_mask(
+                b, t, lens[...]
+            )
+            return acc + jnp.sum(v * v, axis=0)
+
+        m2 = jnp.sum(
+            lax.fori_loop(0, 8, spread, jnp.zeros((8, HALF), F32)), axis=0, keepdims=True
+        )
+        return mean, m2
+
+    def layer_step(layer, _):
+        pltpu.make_async_copy(
+            W.at[pl.ds(17 * layer, 17)], w_out.at[pl.ds(17 * layer, 17)], out_s.at[layer]
+        ).start()
+        pltpu.make_async_copy(
+            hA.at[layer, :, pl.ds(HALO, ROWS)], h_out.at[layer], out_s.at[5 + layer]
+        ).start()
+
+        acc = jnp.zeros((ROWS, HALF), F32)
+        for k in range(17):
+            for h in range(2):
+                lhs = (
+                    hA[layer, h, pl.ds(8 * k, ROWS), :]
+                    if k % 2 == 0
+                    else hB[h, pl.ds(8 * (k - 1), ROWS), :]
+                )
+                acc = acc + jnp.dot(
+                    lhs,
+                    W[17 * layer + k, pl.ds(8 * h, 8)].reshape(HALF, HALF),
+                    preferred_element_type=F32,
+                )
+        z[...] = acc
+
+        @pl.when(layer == 1)
+        def _():
+            for j in range(3):
+                zb[j] = jnp.dot(nar[j], wmn[j], preferred_element_type=F32)
+
+        @pl.when(layer == 2)
+        def _():
+            zb[0] = jnp.dot(
+                wid[0], wmw[0, pl.ds(0, HALF), :], preferred_element_type=F32
+            ) + jnp.dot(wid[1], wmw[0, pl.ds(HALF, HALF), :], preferred_element_type=F32)
+            zb[1] = jnp.dot(
+                hA[0, 0, pl.ds(HALO, ROWS), :],
+                wmw[1, pl.ds(0, HALF), :],
+                preferred_element_type=F32,
+            ) + jnp.dot(
+                hA[0, 1, pl.ds(HALO, ROWS), :],
+                wmw[1, pl.ds(HALF, HALF), :],
+                preferred_element_type=F32,
+            )
+
+        def put_stats(ref, field):
+            mean, m2 = local_stats(ref)
+            st[layer, t, pl.ds(2 * field, 1), :] = mean
+            st[layer, t, pl.ds(2 * field + 1, 1), :] = m2
+
+        st[layer, t] = jnp.zeros((8, HALF), F32)
+        put_stats(z, 0)
+        for at, number in ((1, 3), (2, 2)):
+
+            @pl.when(layer == at)
+            def _():
+                for j in range(number):
+                    put_stats(zb.at[j], 1 + j)
+
+        share(st, layer, t, x, st_s.at[layer], st_r.at[layer])
+        wait_on(st.at[layer, pl.ds(0, 15)], st_r.at[layer])
+        zero = jnp.zeros((8, HALF), F32)
+        count = lax.fori_loop(0, 16, lambda s, a: a + nv[s], zero)
+        mean = lax.fori_loop(0, 16, lambda s, a: a + nv[s] * st[layer, s], zero) / count
+
+        def gather_spread(s, a):
+            v = st[layer, s]
+            d = v - mean
+            return a[0] + nv[s] * d * d, a[1] + v
+
+        between, inside = lax.fori_loop(0, 16, gather_spread, (zero, zero))
+
+        def moments(field):
+            m = mean[2 * field : 2 * field + 1]
+            q = (inside[2 * field + 1 : 2 * field + 2] + between[2 * field : 2 * field + 1]) / count[:1]
+            return m, lax.rsqrt(q + EPS)
+
+        def branches(base, number):
+            for j in range(number):
+                m, r = moments(1 + j)
+                field = base + j
+                rs_out[field] = jnp.broadcast_to(r, (8, HALF))
+                gain = norm[field, pl.ds(0, 1), :]
+                bias = norm[field, pl.ds(1, 1), :]
+                if j > 0:
+                    wait_on(xhb.at[1], out_s.at[10])
+
+                def one(b, _):
+                    v = (zb[j, rows_of(b), :] - m) * r
+                    xhb[1, rows_of(b), :] = v
+                    y = gain * v + bias
+                    if field > 5:
+                        y = y + y5[rows_of(b), :]
+                    y5[rows_of(b), :] = y
+                    return 0
+
+                lax.fori_loop(0, 8, one, 0)
+                pltpu.make_async_copy(xhb.at[1], xh_out.at[field], out_s.at[10]).start()
+            wait_on(xhb.at[1], out_s.at[10])
+
+        m, r = moments(0)
+        rs_out[layer] = jnp.broadcast_to(r, (8, HALF))
+        gain = norm[layer, pl.ds(0, 1), :]
+        bias = norm[layer, pl.ds(1, 1), :]
+
+        @pl.when(layer > 0)
+        def _():
+            wait_on(xhb.at[0], out_s.at[11])
+
+        @pl.when(layer < 4)
+        def _():
+            def one(b, _):
+                v = (z[rows_of(b), :] - m) * r
+                xhb[0, rows_of(b), :] = v
+                y = gain * v + bias
+                a = (y * jax.nn.sigmoid(y)).reshape(16, 8, HALF) * frame_mask(b, t, lens[...])
+                hA[layer + 1, x, pl.ds(pl.multiple_of(HALO + b * 128, 64), 128), :] = a.reshape(
+                    128, HALF
+                ).astype(BF)
+                return 0
+
+            lax.fori_loop(0, 8, one, 0)
+
+            @pl.when(t > 0)
+            def _():
+                for to in range(2):
+                    a = hA.at[layer + 1, x, pl.ds(HALO, HALO)]
+                    b = hA.at[layer + 1, x, pl.ds(1088, HALO)]
+                    remote(
+                        a,
+                        b,
+                        halo_s.at[layer + 1, 0, to],
+                        halo_r.at[layer + 1, 0, x],
+                        (t - 1, x if to == 0 else 1 - x),
+                    )
+
+            @pl.when(t < 15)
+            def _():
+                for to in range(2):
+                    a = hA.at[layer + 1, x, pl.ds(1024, HALO)]
+                    b = hA.at[layer + 1, x, pl.ds(0, HALO)]
+                    remote(
+                        a,
+                        b,
+                        halo_s.at[layer + 1, 1, to],
+                        halo_r.at[layer + 1, 1, x],
+                        (t + 1, x if to == 0 else 1 - x),
+                    )
+
+            inner = hA.at[layer + 1, x, pl.ds(HALO, ROWS)]
+            remote(inner, inner, x_s.at[layer], x_r.at[layer], partner)
+
+        @pl.when(layer == 4)
+        def _():
+            def one(b, _):
+                v = (z[rows_of(b), :] - m) * r
+                xhb[0, rows_of(b), :] = v
+                y5[rows_of(b), :] = y5[rows_of(b), :] + gain * v + bias
+                return 0
+
+            lax.fori_loop(0, 8, one, 0)
+
+        pltpu.make_async_copy(xhb.at[0], xh_out.at[layer], out_s.at[11]).start()
+
+        @pl.when(layer < 4)
+        def _():
+            serve(11 + 7 * layer, 18 + 7 * layer)
+
+        @pl.when(layer == 0)
+        def _():
+            copies[13].wait()
+            wait_on(rawn.at[0], xr_r.at[2])
+            for j in range(3):
+                for s in range(8):
+                    spread_half(rawn[s // 4, j, s % 4], s)
+
+                def one(b, _):
+                    nar[j, rows_of(b), :] = masked_block(b, 0)
+                    return 0
+
+                lax.fori_loop(0, 8, one, 0)
+
+        @pl.when(layer == 1)
+        def _():
+            branches(5, 3)
+            wait_on(raww.at[0, 0], xr_r.at[3])
+            spread_wide(0)
+
+            def one(b, _):
+                for h in range(2):
+                    wid[h, rows_of(b), :] = masked_block(b, h)
+                return 0
+
+            lax.fori_loop(0, 8, one, 0)
+
+        @pl.when(layer == 2)
+        def _():
+            branches(8, 2)
+            copies[14].wait()
+            remote(cot.at[:, :, other], rawc.at[x], xr_s.at[4], xr_r.at[4], partner)
+
+        @pl.when(layer == 3)
+        def _():
+            wait_on(rawc.at[0], xr_r.at[4])
+            for s in range(8):
+                spread_half(rawc[s // 4, s % 4], s)
+
+            def one(b, _):
+                cotv[rows_of(b), :] = masked_block(b, 0)
+                return 0
+
+            lax.fori_loop(0, 8, one, 0)
+
+        @pl.when(layer < 4)
+        def _():
+            wait_on(hA.at[0, 0, pl.ds(HALO, ROWS)], x_r.at[layer])
+            halo_wait(layer + 1, False)
+            shift_copy(layer + 1)
+
+        return 0
+
+    lax.fori_loop(0, 5, layer_step, 0)
+
+    last = [
+        (wmn, wmn_out),
+        (wmw, wmw_out),
+        (y5, y_out),
+        (nar, nar_out),
+        (wid, wid_out),
+        (cotv, cot_out),
+    ]
+    for i, (a, b) in enumerate(last):
+        pltpu.make_async_copy(a, b, out_s.at[12 + i]).start()
+    for i, (a, b) in enumerate(last):
+        wait_on(a, out_s.at[12 + i])
+    wait_on(xhb.at[0], out_s.at[11])
+    for i in range(5):
+        wait_on(W.at[pl.ds(0, 17)], out_s.at[i])
+        wait_on(hA.at[0, :, pl.ds(HALO, ROWS)], out_s.at[5 + i])
+
+    def drained(g, _):
+        wait_on(amount(g, 15), ag_s.at[g])
+        return 0
+
+    lax.fori_loop(0, GROUPS, drained, 0)
+    wait_on(G.at[pl.ds(0, 15)], m_s)
+    wait_on(lenr.at[0], xr_s.at[0])
+    wait_on(raww.at[0, 1], xr_s.at[1])
+    wait_on(rawn.at[0], xr_s.at[2])
+    wait_on(raww.at[0, 0], xr_s.at[3])
+    wait_on(rawc.at[0], xr_s.at[4])
+
+    def finish(layer, _):
+        halo_wait(layer, True)
+        wait_on(st.at[layer, pl.ds(0, 15)], st_s.at[layer])
+
+        @pl.when(layer < 4)
+        def _():
+            wait_on(hA.at[0, 0, pl.ds(HALO, ROWS)], x_s.at[layer])
+
+        return 0
+
+    lax.fori_loop(0, 5, finish, 0)
+
+
+def run_forward(lens, norm, perm, src_n, src_w, cot, kf, kr, mn, mw):
+    vm = pl.BlockSpec(memory_space=pltpu.VMEM)
+    hb = pl.BlockSpec(memory_space=pl.ANY)
+    dma = pltpu.SemaphoreType.DMA
+    S = jax.ShapeDtypeStruct
+    return pl.pallas_call(
+        forward_kernel,
+        out_shape=(
+            S((85, 16, 32, HALF), BF),
+            S((3, HALF, HALF), BF),
+            S((2, 512, HALF), BF),
+            S((5, 2, ROWS, HALF), BF),
+            S((10, ROWS, HALF), F32),
+            S((ROWS, HALF), F32),
+            S((3, ROWS, HALF), BF),
+            S((2, ROWS, HALF), BF),
+            S((ROWS, HALF), BF),
+            S((10, 8, HALF), F32),
+            S((8, HALF), F32),
+        ),
+        in_specs=[vm, vm, vm] + [hb] * 7,
+        out_specs=[hb] * 9 + [vm, vm],
+        scratch_shapes=[
+            pltpu.VMEM((85, 16, 32, HALF), BF),
+            pltpu.VMEM((16, 112, HALF), BF),
+            pltpu.VMEM((3, HALF, HALF), BF),
+            pltpu.VMEM((2, 512, HALF), BF),
+            pltpu.VMEM((5, 2, 1168, HALF), BF),
+            pltpu.VMEM((2, 1152, HALF), BF),
+            pltpu.VMEM((ROWS, HALF), F32),
+            pltpu.VMEM((3, ROWS, HALF), F32),
+            pltpu.VMEM((2, ROWS, HALF), F32),
+            pltpu.VMEM((ROWS, HALF), F32),
+            pltpu.VMEM((4, ROWS, 128), F32),
+            pltpu.VMEM((5, 2, 544, 128), F32),
+            pltpu.VMEM((3, 16, HALF), F32),
+            pltpu.VMEM((2, 24, HALF), F32),
+            pltpu.VMEM((2, 2, 4, 128, 384), BF),
+            pltpu.VMEM((2, 3, 4, 128, HALF), BF),
+            pltpu.VMEM((2, 4, 128, HALF), BF),
+            pltpu.VMEM((3, ROWS, HALF), BF),
+            pltpu.VMEM((2, ROWS, HALF), BF),
+            pltpu.VMEM((ROWS, HALF), BF),
+            pltpu.VMEM((5, 16, 8, HALF), F32),
+            pltpu.VMEM((16, 8, HALF), F32),
+            pltpu.VMEM((2, 8, HALF), F32),
+            pltpu.VMEM((8, HALF), F32),
+            dma((15,)),
+            dma((GROUPS,)),
+            dma((GROUPS,)),
+            dma((GROUPS,)),
+            dma((GROUPS,)),
+            dma,
+            dma((3,)),
+            dma((4,)),
+            dma((4,)),
+            dma((5,)),
+            dma((5,)),
+            dma((5, 2, 2)),
+            dma((5, 2, 2)),
+            dma((5,)),
+            dma((5,)),
+            dma((18,)),
+        ],
+        compiler_params=pltpu.CompilerParams(
+            collective_id=0, has_side_effects=True, vmem_limit_bytes=62 << 20
+        ),
+        cost_estimate=pl.CostEstimate(flops=24 * 10**9, bytes_accessed=60 * 10**6, transcendentals=0),
+    )(lens, norm, perm, src_n, src_w, cot, kf, kr, mn, mw)
+
+
+def backward_kernel(
+    lens_in,
+    norm,
+    rs,
+    perm,
+    w_in,
+    wmn,
+    wmw,
+    h_in,
+    xh_in,
+    y_in,
+    nar_in,
+    wid_in,
+    cot_in,
+    mixed_out,
+    gn_out,
+    gw_out,
+    gf_out,
+    gr_out,
+    gmn_out,
+    gmw_out,
+    ng_out,
+    total_out,
+    Wl,
+    Hl,
+    Xl,
+    xb,
+    sb,
+    y5,
+    da,
+    dzA,
+    dzB,
+    dW,
+    crecv,
+    yrecv,
+    zrecv,
+    fin,
+    xrecv,
+    px,
+    pxr,
+    stg,
+    own_n,
+    own_w,
+    snd_n,
+    snd_w,
+    rcv_n,
+    rcv_w,
+    mix_own,
+    mix_rcv,
+    Dm,
+    cm,
+    ym,
+    zm,
+    fm,
+    xm,
+    gst,
+    gsm,
+    bst,
+    ngr,
+    ngx,
+    ss,
+    fst,
+    load_s,
+    w_s,
+    go,
+    br_s,
+    halo_s,
+    halo_r,
+    st_s,
+    st_r,
+    c_s,
+    c_r,
+    y_s,
+    y_r,
+    z_s,
+    z_r,
+    f_s,
+    f_r,
+    px_s,
+    px_r,
+    m_s,
+    m_r,
+    sn_s,
+    sn_r,
+    g_s,
+    out_s,
+    ng_s,
+    ng_r,
+):
+    x, t, zi, yi, ci = position()
+    partner = (t, 1 - x)
+    sibling = (t + 1 - 2 * ci, x)
+    across = (zi * 4 + (1 - yi) * 2 + ci, x)
+    lens = lens_in[...]
+
+    def when(cond, f):
+        if isinstance(cond, bool):
+            if cond:
+                f()
+        else:
+            pl.when(cond)(f)
+
+    def rows_of(b):
+        return pl.ds(pl.multiple_of(b * 128, 128), 128)
+
+    def copy_in(src, dst, sem):
+        pltpu.make_async_copy(src, dst, sem).start()
+
+    def load_w(layer):
+        b2 = lax.rem(layer, 2)
+        copy_in(w_in.at[pl.ds(17 * layer, 17)], Wl.at[b2], w_s.at[b2])
+
+    def load_h(layer):
+        copy_in(h_in.at[layer], Hl, load_s.at[1])
+
+    def load_x(layer):
+        copy_in(xh_in.at[layer], Xl, load_s.at[2])
+
+    copy_in(y_in, y5, load_s.at[3])
+    copy_in(cot_in, sb.at[0], load_s.at[4])
+    load_x(4)
+    copy_in(xh_in.at[5], xb.at[1], br_s.at[1])
+    load_w(4)
+    load_h(4)
+
+    for edge, lo in ((0, 0), (15, 1088)):
+
+        @pl.when(t == edge)
+        def _():
+            dzA[:, pl.ds(lo, HALO), :] = jnp.zeros((2, HALO, HALF), BF)
+
+    dzA[:, pl.ds(1152, 16), :] = jnp.zeros((2, 16, HALF), BF)
+    barrier = pltpu.get_barrier_semaphore()
+
+    def greet_one(d, _):
+        pl.semaphore_signal(
+            barrier, inc=1, device_id=(lax.rem(t + d, 16), x), device_id_type=MESH
+        )
+        return 0
+
+    lax.fori_loop(1, 16, greet_one, 0)
+    pl.semaphore_signal(barrier, inc=1, device_id=partner, device_id_type=MESH)
+    pl.semaphore_wait(barrier, 16)
+
+    zero = jnp.zeros((8, HALF), F32)
+    count = jnp.zeros((1, HALF), F32)
+    for s in range(16):
+        count = count + jnp.sum(jnp.clip(lens - 128.0 * s, 0.0, 128.0), axis=0, keepdims=True)
+
+    def mask(b):
+        return frame_mask(b, t, lens)
+
+    def sequence(block, s):
+        return stg[block, pl.ds(s, 128, stride=8), :]
+
+    def unstage(blocks, own, send):
+        for i in range(4):
+            for b in range(blocks):
+                own(i, b, sequence(b, 4 * x + i))
+                send(i, b, sequence(b, 4 * (1 - x) + i))
+
+    wait_on(y5, load_s.at[3])
+
+    def out_block(b, _):
+        y = y5[rows_of(b), :]
+        a = (y * jax.nn.sigmoid(y)).reshape(16, 8, HALF) * mask(b)
+        a = a.reshape(128, HALF)
+        for i in range(2):
+            stg[i, rows_of(b), :] = a[:, 128 * i : 128 * i + 128]
+        return 0
+
+    lax.fori_loop(0, 8, out_block, 0)
+
+    def mix_put(ref):
+        def put(i, b, v):
+            ref[i, :, pl.ds(128 * b, 128)] = v.astype(BF)
+
+        return put
+
+    unstage(2, mix_put(mix_own.at[0]), mix_put(mix_own.at[1]))
+    remote(mix_own.at[1], mix_rcv, sn_s.at[0], sn_r.at[0], partner)
+    my_cols = pl.ds(pl.multiple_of(x * HALF, HALF), HALF)
+    other_cols = pl.ds(pl.multiple_of((1 - x) * HALF, HALF), HALF)
+    copy_in(mix_own.at[0], mixed_out.at[:, :, my_cols], out_s.at[0])
+
+    wait_on(sb.at[0], load_s.at[4])
+
+    def start_da(b, _):
+        da[rows_of(b), :] = sb[0, rows_of(b), :].astype(F32)
+        return 0
+
+    lax.fori_loop(0, 8, start_da, 0)
+
+    def slot_z(q):
+        return lax.rem(zi + 1 + q, 4)
+
+    def send_core(layer):
+        b3, b2 = lax.rem(layer, 3), lax.rem(layer, 2)
+        for q in range(4):
+            zz = slot_z(q)
+            remote(
+                dW.at[b3, :, zz, :, 1 - ci],
+                crecv.at[b2, :, zz],
+                c_s.at[layer],
+                c_r.at[layer, q],
+                sibling,
+            )
+
+    def add_core(layer, q):
+        b3, b2 = lax.rem(layer, 3), lax.rem(layer, 2)
+        zz = slot_z(q)
+        wait_on(crecv.at[b2, :, zz], c_r.at[layer, q])
+        for yy in range(2):
+
+            def one(k, _):
+                dW[b3, k, zz, yy, ci] = (
+                    dW[b3, k, zz, yy, ci].astype(F32) + crecv[b2, k, zz, yy].astype(F32)
+                ).astype(BF)
+                return 0
+
+            lax.fori_loop(0, 17, one, 0)
+        remote(
+            dW.at[b3, :, zz, 1 - yi, ci],
+            yrecv.at[b2, :, zz],
+            y_s.at[layer],
+            y_r.at[layer, q],
+            across,
+        )
+
+    def add_across(layer, q):
+        b3, b2 = lax.rem(layer, 3), lax.rem(layer, 2)
+        zz = slot_z(q)
+        wait_on(yrecv.at[b2, :, zz], y_r.at[layer, q])
+
+        def one(k, _):
+            dW[b3, k, zz, yi, ci] = (
+                dW[b3, k, zz, yi, ci].astype(F32) + yrecv[b2, k, zz].astype(F32)
+            ).astype(BF)
+            return 0
+
+        lax.fori_loop(0, 17, one, 0)
+        if q < 3:
+            remote(
+                dW.at[b3, :, zz, yi, ci],
+                zrecv.at[b2, q],
+                z_s.at[layer],
+                z_r.at[layer],
+                (zz * 4 + yi * 2 + ci, x),
+            )
+
+    def finish_sum(layer):
+        b3, b2 = lax.rem(layer, 3), lax.rem(layer, 2)
+        wait_on(zrecv.at[b2], z_r.at[layer])
+        when(layer + 2 <= 4, lambda: wait_on(fin.at[0], f_s.at[layer + 2]))
+
+        def one(k, _):
+            v = dW[b3, k, zi, yi, ci].astype(F32)
+            for q in range(3):
+                v = v + zrecv[b2, q, k].astype(F32)
+            fin[b2, k] = v.astype(BF)
+            return 0
+
+        lax.fori_loop(0, 17, one, 0)
+        remote(fin.at[b2], xrecv.at[layer], f_s.at[layer], f_r.at[layer], partner)
+
+    def add_square(v):
+        ss[...] += jnp.sum((v * v).reshape(-1, 8, 128), axis=0)
+
+    def assemble(layer, rows, put):
+        b2 = lax.rem(layer, 2)
+        wait_on(xrecv.at[layer], f_r.at[layer])
+        for k in range(17):
+            for b in range(2):
+                lanes = pl.ds(128 * b, 128)
+                gst[2 * x + b, pl.ds(k, rows, stride=17), :] = fin[
+                    b2, k, pl.ds(0, 32), lanes
+                ].astype(F32)[:rows]
+                gst[2 * (1 - x) + b, pl.ds(k, rows, stride=17), :] = xrecv[
+                    layer, k, pl.ds(0, 32), lanes
+                ].astype(F32)[:rows]
+        for b in range(4):
+            add_square(gst[b, pl.ds(0, rows * 17), :])
+            copy_in(gst.at[b, pl.ds(0, rows * 17)], put(b), g_s)
+
+    def wait_assembled(rows):
+        wait_on(gst.at[:, pl.ds(0, rows * 17)], g_s)
+
+    def drain_sums(layer):
+        wait_on(crecv.at[0], c_s.at[layer])
+        wait_on(yrecv.at[0], y_s.at[layer])
+        wait_on(zrecv.at[0], z_s.at[layer])
+
+    def put_rest(layer):
+        return lambda b: gr_out.at[layer - 1, :, pl.ds(128 * b, 128)]
+
+    def mixers_one():
+        remote(Dm.at[:, :, 1 - ci], cm, m_s.at[0], m_r.at[0], sibling)
+
+    def mixers_two():
+        wait_on(cm, m_r.at[0])
+        for zz in range(4):
+            for yy in range(2):
+                Dm[zz, yy, ci] = (Dm[zz, yy, ci].astype(F32) + cm[zz, yy].astype(F32)).astype(BF)
+        remote(Dm.at[:, 1 - yi, ci], ym, m_s.at[1], m_r.at[1], across)
+
+    def mixers_three():
+        wait_on(ym, m_r.at[1])
+        for zz in range(4):
+            Dm[zz, yi, ci] = (Dm[zz, yi, ci].astype(F32) + ym[zz].astype(F32)).astype(BF)
+        for q in range(3):
+            zz = slot_z(q)
+            remote(Dm.at[zz, yi, ci], zm.at[q], m_s.at[2], m_r.at[2], (zz * 4 + yi * 2 + ci, x))
+
+    def mixers_four():
+        wait_on(zm, m_r.at[2])
+        v = Dm[zi, yi, ci].astype(F32)
+        for q in range(3):
+            v = v + zm[q].astype(F32)
+        fm[...] = v.astype(BF)
+        remote(fm, xm, m_s.at[3], m_r.at[3], partner)
+
+    def mixers_five():
+        wait_on(xm, m_r.at[3])
+        for b in range(2):
+            lanes = pl.ds(128 * b, 128)
+            gsm[2 * x + b] = fm[:, lanes].astype(F32)
+            gsm[2 * (1 - x) + b] = xm[:, lanes].astype(F32)
+        for b in range(4):
+            add_square(gsm[b])
+            for j in range(3):
+                copy_in(
+                    gsm.at[b, pl.ds(16 * j, 16)],
+                    gmn_out.at[j, :, pl.ds(128 * b, 128)],
+                    out_s.at[1],
+                )
+            for j in range(2):
+                copy_in(
+                    gsm.at[b, pl.ds(48 + 32 * j, 24)],
+                    gmw_out.at[j, :, pl.ds(128 * b, 128)],
+                    out_s.at[2],
+                )
+
+    def halo_sent(layer):
+        for side, edge in ((0, 0), (1, 15)):
+
+            @pl.when(t != edge)
+            def _():
+                wait_on(dzA.at[0, pl.ds(0, HALO)], halo_s.at[layer, side])
+
+    def norm_backward(layer, last):
+        wait_on(Xl, load_s.at[2])
+        gain = norm[layer, pl.ds(0, 1), :]
+        bias = norm[layer, pl.ds(1, 1), :]
+
+        def one(b, acc):
+            xh = Xl[rows_of(b), :]
+            y = y5[rows_of(b), :] if last else gain * xh + bias
+            sg = jax.nn.sigmoid(y)
+            v = da[rows_of(b), :] * sg * (1.0 + y * (1.0 - sg))
+            v = v.reshape(16, 8, HALF) * mask(b)
+            s0 = acc[0] + jnp.sum(v, axis=0)
+            s1 = acc[1] + jnp.sum(v * xh.reshape(16, 8, HALF), axis=0)
+            v = v.reshape(128, HALF)
+            da[rows_of(b), :] = v
+            if last:
+                y5[rows_of(b), :] = v
+            return s0, s1
+
+        s0, s1 = lax.fori_loop(0, 8, one, (zero, zero))
+        bst[layer, t] = zero
+        bst[layer, t, pl.ds(0, 1), :] = jnp.sum(s0, axis=0, keepdims=True)
+        bst[layer, t, pl.ds(1, 1), :] = jnp.sum(s1, axis=0, keepdims=True)
+        if last:
+            for j in range(5):
+                at = (j + 1) % 2
+                wait_on(xb.at[at], br_s.at[at])
+                if j < 4:
+                    copy_in(xh_in.at[6 + j], xb.at[1 - at], br_s.at[1 - at])
+
+                def branch(b, acc):
+                    return acc + jnp.sum(
+                        (da[rows_of(b), :] * xb[at, rows_of(b), :]).reshape(16, 8, HALF), axis=0
+                    )
+
+                sj = lax.fori_loop(0, 8, branch, zero)
+                bst[layer, t, pl.ds(2 + j, 1), :] = jnp.sum(sj, axis=0, keepdims=True)
+        share(bst, layer, t, x, st_s.at[layer], st_r.at[layer])
+        wait_on(bst.at[layer, pl.ds(0, 15)], st_r.at[layer])
+        sums = lax.fori_loop(0, 16, lambda s, a: a + bst[layer, s], zero)
+        ngr[layer, pl.ds(0, 1), :] = sums[1:2]
+        ngr[layer, pl.ds(1, 1), :] = sums[0:1]
+        if last:
+            for j in range(5):
+                ngr[5 + j, pl.ds(0, 1), :] = sums[2 + j : 3 + j]
+                ngr[5 + j, pl.ds(1, 1), :] = sums[0:1]
+        r = rs[layer, pl.ds(0, 1), :]
+        c0 = gain * sums[0:1] / count
+        c1 = gain * sums[1:2] / count
+        b2 = lax.rem(layer, 2)
+
+        def dz_block(b, _):
+            m = mask(b)
+            v = (gain * da[rows_of(b), :]).reshape(16, 8, HALF)
+            xh = Xl[rows_of(b), :].reshape(16, 8, HALF)
+            v = r * (v - m * c0 - m * xh * c1)
+            dzA[b2, pl.ds(pl.multiple_of(HALO + b * 128, 64), 128), :] = v.reshape(
+                128, HALF
+            ).astype(BF)
+            return 0
+
+        when(layer + 2 <= 4, lambda: halo_sent(layer + 2))
+        lax.fori_loop(0, 8, dz_block, 0)
+        for side, edge, lo, to in ((0, 0, HALO, 1088), (1, 15, 1024, 0)):
+
+            @pl.when(t != edge)
+            def _():
+                remote(
+                    dzA.at[b2, pl.ds(lo, HALO)],
+                    dzA.at[b2, pl.ds(to, HALO)],
+                    halo_s.at[layer, side],
+                    halo_r.at[layer, side],
+                    (t - 1 + 2 * side, x),
+                )
+
+        return sums
+
+    def halo_arrived(layer):
+        b2 = lax.rem(layer, 2)
+        for side, edge in ((1, 0), (0, 15)):
+
+            @pl.when(t != edge)
+            def _():
+                wait_on(dzA.at[b2, pl.ds(0, HALO)], halo_r.at[layer, side])
+
+        def one(b, _):
+            v = dzA[b2, pl.ds(pl.multiple_of(b * 128, 128), 144), :].astype(F32)
+            dzB[pl.ds(pl.multiple_of(b * 128, 128), 128), :] = v[8:136].astype(BF)
+            return 0
+
+        lax.fori_loop(0, 9, one, 0)
+
+    def shifted(b2, k):
+        o = 16 - k
+        if o % 2 == 0:
+            return dzA[b2, pl.ds(8 * o, ROWS), :]
+        return dzB[pl.ds(8 * (o - 1), ROWS), :]
+
+    def data_half(layer, half):
+        b2 = lax.rem(layer, 2)
+        acc = jnp.zeros((ROWS, HALF), F32)
+        for k in range(17):
+            acc = acc + lax.dot_general(
+                shifted(b2, k),
+                Wl[b2, k, pl.ds(8 * half, 8)].reshape(HALF, HALF),
+                (((1,), (1,)), ((), ())),
+                preferred_element_type=F32,
+            )
+        return acc
+
+    def weight_gradient(layer):
+        b3, b2 = lax.rem(layer, 3), lax.rem(layer, 2)
+        wait_on(Hl, load_s.at[1])
+        for k in range(17):
+            for h in range(2):
+                v = lax.dot_general(
+                    Hl[h], shifted(b2, k), (((0,), (0,)), ((), ())), preferred_element_type=F32
+                )
+                dW[b3, k, pl.ds(2 * h, 2)] = v.reshape(2, 2, 2, 32, HALF).astype(BF)
+
+    def branches(sums):
+        own_first = True
+        for j in range(5):
+            field = 5 + j
+            copy_in(xh_in.at[field], xb.at[0], br_s.at[0])
+            if j < 3:
+                copy_in(nar_in.at[j], sb.at[0], br_s.at[2])
+            elif j == 3:
+                copy_in(wid_in, sb, br_s.at[2])
+            else:
+                copy_in(h_in.at[0], sb, br_s.at[2])
+            wait_on(xb.at[0], br_s.at[0])
+            wait_on(sb.at[0] if j < 3 else sb, br_s.at[2])
+            gain = norm[field, pl.ds(0, 1), :]
+            r = rs[field, pl.ds(0, 1), :]
+            c0 = gain * sums[0:1] / count
+            c1 = gain * sums[2 + j : 3 + j] / count
+
+            def one(b, _):
+                m = mask(b)
+                v = (gain * y5[rows_of(b), :]).reshape(16, 8, HALF)
+                xh = xb[0, rows_of(b), :].reshape(16, 8, HALF)
+                v = r * (v - m * c0 - m * xh * c1)
+                px[1, rows_of(b), :] = v.reshape(128, HALF).astype(BF)
+                return 0
+
+            lax.fori_loop(0, 8, one, 0)
+            dv = px[1]
+            if j < 3:
+                v = lax.dot_general(
+                    sb[0], dv, (((0,), (0,)), ((), ())), preferred_element_type=F32
+                )
+                Dm[:, :, :, pl.ds(16 * j, 16), :] = v.reshape(4, 2, 2, 16, HALF).astype(BF)
+                back = lax.dot_general(
+                    dv, wmn[j], (((1,), (1,)), ((), ())), preferred_element_type=F32
+                )
+                blocks = 2
+            else:
+                i = j - 3
+                for h in range(2):
+                    v = lax.dot_general(
+                        sb[h], dv, (((0,), (0,)), ((), ())), preferred_element_type=F32
+                    )
+                    Dm[pl.ds(2 * h, 2), :, :, pl.ds(48 + 32 * i, 32), :] = v.reshape(
+                        2, 2, 2, 32, HALF
+                    ).astype(BF)
+                wu = jnp.dot(perm[...], wmw[i], preferred_element_type=F32).astype(BF)
+                back = lax.dot_general(
+                    dv, wu, (((1,), (1,)), ((), ())), preferred_element_type=F32
+                )
+                blocks = 3
+            for b in range(blocks):
+                stg[b] = back[:, 128 * b : 128 * b + 128]
+
+            def masked(b, _):
+                m = mask(b)[:, :, :128]
+                for i in range(blocks):
+                    stg[i, rows_of(b), :] = (
+                        stg[i, rows_of(b), :].reshape(16, 8, 128) * m
+                    ).reshape(128, 128)
+                return 0
+
+            lax.fori_loop(0, 8, masked, 0)
+            if j < 3:
+
+                def put_own(i, b, v):
+                    own_n[j, i, :, pl.ds(128 * b, 128)] = v
+
+                def put_send(i, b, v):
+                    snd_n[j, i, :, pl.ds(128 * b, 128)] = v.astype(BF)
+
+            else:
+
+                def put_own(i, b, v):
+                    own_w[j - 3, i, :, pl.ds(128 * b, 128)] = v
+
+                def put_send(i, b, v):
+                    snd_w[j - 3, i, :, pl.ds(128 * b, 128)] = v.astype(BF)
+
+            unstage(blocks, put_own, put_send)
+        remote(snd_n, rcv_n, sn_s.at[1], sn_r.at[1], partner)
+        remote(snd_w.at[pl.ds(0, 2)], rcv_w.at[pl.ds(0, 2)], sn_s.at[2], sn_r.at[2], partner)
+
+    def sources_narrow():
+        wait_on(rcv_n, sn_r.at[1])
+        own_n[...] = own_n[...] + rcv_n[...].astype(F32)
+        copy_in(own_n, gn_out, out_s.at[3])
+
+    def chain(layer, last, first):
+        load_next = lambda f: when(layer > 0, lambda: f(layer - 1))
+        b2 = lax.rem(layer, 2)
+        load_next(load_w)
+        sums = norm_backward(layer, last)
+        load_next(load_x)
+        halo_arrived(layer)
+
+        if last is False:
+
+            def finish_older():
+                add_across(layer + 2, 2)
+                add_across(layer + 2, 3)
+
+            when(layer + 2 <= 4, finish_older)
+            for q in range(4):
+                add_core(layer + 1, q)
+        wait_on(Wl.at[0], w_s.at[b2])
+        if first is False:
+            if last is False:
+                wait_on(px.at[0], px_s)
+            acc = data_half(layer, 1 - x)
+            px[0] = acc.astype(BF)
+            remote(px.at[0], pxr.at[b2], px_s, px_r.at[layer], partner)
+            da[...] = data_half(layer, x)
+        if last is False:
+            when(layer + 2 <= 4, lambda: finish_sum(layer + 2))
+            if first:
+                for to in [across] + [(slot_z(q) * 4 + yi * 2 + ci, x) for q in range(3)]:
+                    pl.semaphore_signal(go, inc=1, device_id=to, device_id_type=MESH)
+            add_across(layer + 1, 0)
+            when(layer + 3 <= 4, lambda: drain_sums(layer + 3))
+        weight_gradient(layer)
+        load_next(load_h)
+        if last is False:
+            add_across(layer + 1, 1)
+        send_core(layer)
+        if last is False:
+
+            def older_out():
+                when(layer + 3 <= 4, lambda: wait_assembled(32))
+                assemble(layer + 2, 32, put_rest(layer + 2))
+
+            when(layer + 2 <= 4, older_out)
+        if last:
+            branches(sums)
+        if first is False:
+            wait_on(pxr.at[0], px_r.at[layer])
+
+            def one(b, _):
+                da[rows_of(b), :] = da[rows_of(b), :] + pxr[b2, rows_of(b), :].astype(F32)
+                return 0
+
+            lax.fori_loop(0, 8, one, 0)
+
+    ss[...] = jnp.zeros((8, 128), F32)
+    chain(4, True, False)
+    mixers_one()
+    mixers_two()
+
+    def middle(i, _):
+        layer = 3 - i
+        chain(layer, False, False)
+
+        @pl.when(layer == 3)
+        def _():
+            mixers_three()
+            wait_on(mix_rcv, sn_r.at[0])
+            copy_in(mix_rcv, mixed_out.at[:, :, other_cols], out_s.at[4])
+
+        @pl.when(layer == 2)
+        def _():
+            mixers_four()
+            sources_narrow()
+
+        @pl.when(layer == 1)
+        def _():
+            mixers_five()
+
+        return 0
+
+    lax.fori_loop(0, 3, middle, 0)
+    chain(0, False, True)
+
+    remote(ngr, ngx, ng_s, ng_r, partner)
+
+    for k in range(17):
+        Wl[1, k, pl.ds(0, 12)] = (
+            jnp.dot(perm[...], Wl[0, k].reshape(512, HALF), preferred_element_type=F32)
+            .astype(BF)
+            .reshape(12, 32, HALF)
+        )
+    add_across(1, 2)
+    pl.semaphore_wait(go, 4)
+    add_core(0, 0)
+    add_core(0, 1)
+    add_across(1, 3)
+    add_core(0, 2)
+    add_core(0, 3)
+    for part in range(4):
+        acc = jnp.zeros((HALF, 384), F32)
+        for k in range(17):
+            o = 16 - k
+            lo = part * HALF
+            lhs = (
+                dzA[0, pl.ds(8 * o + lo, HALF), :]
+                if o % 2 == 0
+                else dzB[pl.ds(8 * (o - 1) + lo, HALF), :]
+            )
+            acc = acc + lax.dot_general(
+                lhs,
+                Wl[1, k, pl.ds(0, 12)].reshape(384, HALF),
+                (((1,), (1,)), ((), ())),
+                preferred_element_type=F32,
+            )
+        for half in range(2):
+            m = mask(2 * part + half)[:, :, :128]
+            for b in range(3):
+                stg[b, pl.ds(part * HALF + half * 128, 128), :] = (
+                    acc[128 * half : 128 * half + 128, 128 * b : 128 * b + 128].reshape(
+                        16, 8, 128
+                    )
+                    * m
+                ).reshape(128, 128)
+
+    def put_own(i, b, v):
+        lanes = pl.ds(128 * b, 128)
+        own_w[1, i, :, lanes] = own_w[1, i, :, lanes] + v
+
+    def put_send(i, b, v):
+        snd_w[2, i, :, pl.ds(128 * b, 128)] = v.astype(BF)
+
+    unstage(3, put_own, put_send)
+    remote(snd_w.at[2], rcv_w.at[2], sn_s.at[3], sn_r.at[3], partner)
+    add_across(0, 0)
+    finish_sum(1)
+    add_across(0, 1)
+    add_across(0, 2)
+    add_across(0, 3)
+    wait_assembled(32)
+    assemble(1, 32, put_rest(1))
+    wait_on(rcv_w.at[pl.ds(0, 2)], sn_r.at[2])
+    wait_on(rcv_w.at[2], sn_r.at[3])
+    for j in range(2):
+        v = own_w[j] + rcv_w[j].astype(F32)
+        if j == 1:
+            v = v + rcv_w[2].astype(F32)
+        own_w[j] = v
+    copy_in(own_w, gw_out, out_s.at[5])
+    wait_on(ngx, ng_r)
+    finish_sum(0)
+    wait_assembled(32)
+    assemble(0, 24, lambda b: gf_out.at[:, pl.ds(128 * b, 128)])
+
+    fst[t] = ss[...]
+
+    def tell(d, _):
+        remote(fst.at[t], fst.at[t], st_s.at[5], st_r.at[5], (lax.rem(t + d, 16), x))
+        return 0
+
+    lax.fori_loop(1, 16, tell, 0)
+    mine, theirs = ngr[...], ngx[...]
+    left = jnp.where(x == 0, mine, theirs)
+    right = jnp.where(x == 0, theirs, mine)
+    rows = lax.broadcasted_iota(jnp.int32, (10, 8, HALF), 1)
+    left = jnp.where(rows < 2, left, 0.0)
+    right = jnp.where(rows < 2, right, 0.0)
+    ng_out[0] = left
+    ng_out[1] = right
+    norms = jnp.sum(left * left + right * right)
+    wait_on(fst.at[pl.ds(0, 15)], st_r.at[5])
+    every = lax.fori_loop(0, 16, lambda s, a: a + fst[s], jnp.zeros((8, 128), F32))
+    total_out[...] = jnp.zeros((8, 128), F32) + (jnp.sum(every) + norms)
+
+    wait_assembled(24)
+    wait_on(mix_own.at[0], out_s.at[0])
+    wait_on(mix_rcv, out_s.at[4])
+    wait_on(own_n, out_s.at[3])
+    wait_on(own_w, out_s.at[5])
+    wait_on(gsm.at[:, pl.ds(0, 48)], out_s.at[1])
+    wait_on(gsm.at[:, pl.ds(0, 48)], out_s.at[2])
+    wait_on(px.at[0], px_s)
+    wait_on(mix_own.at[1], sn_s.at[0])
+    wait_on(snd_n, sn_s.at[1])
+    wait_on(snd_w.at[pl.ds(0, 2)], sn_s.at[2])
+    wait_on(snd_w.at[2], sn_s.at[3])
+    wait_on(cm, m_s.at[0])
+    wait_on(ym, m_s.at[1])
+    wait_on(zm, m_s.at[2])
+    wait_on(fm, m_s.at[3])
+    wait_on(ngr, ng_s)
+    wait_on(fst.at[pl.ds(0, 15)], st_s.at[5])
+    for layer in (1, 0, 2):
+        drain_sums(layer)
+
+    for layer in range(2):
+        wait_on(fin.at[0], f_s.at[layer])
+        halo_sent(layer)
+
+    def finish(layer, _):
+        wait_on(bst.at[layer, pl.ds(0, 15)], st_s.at[layer])
+        return 0
+
+    lax.fori_loop(0, 5, finish, 0)
+
+
+def run_backward(lens, norm, rs, perm, w, wmn, wmw, h, xh, y, nar, wid, cot):
+    vm = pl.BlockSpec(memory_space=pltpu.VMEM)
+    hb = pl.BlockSpec(memory_space=pl.ANY)
+    dma = pltpu.SemaphoreType.DMA
+    S = jax.ShapeDtypeStruct
+    V = pltpu.VMEM
+    return pl.pallas_call(
+        backward_kernel,
+        out_shape=(
+            S((4, 128, 512), BF),
+            S((3, 4, 128, HALF), F32),
+            S((2, 4, 128, 384), F32),
+            S((408, 512), F32),
+            S((4, 544, 512), F32),
+            S((3, 16, 512), F32),
+            S((2, 24, 512), F32),
+            S((2, 10, 8, HALF), F32),
+            S((8, 128), F32),
+        ),
+        in_specs=[vm, vm, vm, vm, hb, vm, vm, hb, hb, hb, hb, hb, hb],
+        out_specs=[hb] * 7 + [vm, vm],
+        scratch_shapes=[
+            V((2, 17, 16, 32, HALF), BF),
+            V((2, ROWS, HALF), BF),
+            V((ROWS, HALF), F32),
+            V((2, ROWS, HALF), F32),
+            V((2, ROWS, HALF), BF),
+            V((ROWS, HALF), F32),
+            V((ROWS, HALF), F32),
+            V((2, 1168, HALF), BF),
+            V((1152, HALF), BF),
+            V((3, 17, 4, 2, 2, 32, HALF), BF),
+            V((2, 17, 4, 2, 32, HALF), BF),
+            V((2, 17, 4, 32, HALF), BF),
+            V((2, 3, 17, 32, HALF), BF),
+            V((2, 17, 32, HALF), BF),
+            V((5, 17, 32, HALF), BF),
+            V((2, ROWS, HALF), BF),
+            V((2, ROWS, HALF), BF),
+            V((3, ROWS, 128), F32),
+            V((3, 4, 128, HALF), F32),
+            V((2, 4, 128, 384), F32),
+            V((3, 4, 128, HALF), BF),
+            V((3, 4, 128, 384), BF),
+            V((3, 4, 128, HALF), BF),
+            V((3, 4, 128, 384), BF),
+            V((2, 4, 128, HALF), BF),
+            V((4, 128, HALF), BF),
+            V((4, 2, 2, 112, HALF), BF),
+            V((4, 2, 112, HALF), BF),
+            V((4, 112, HALF), BF),
+            V((3, 112, HALF), BF),
+            V((112, HALF), BF),
+            V((112, HALF), BF),
+            V((4, 544, 128), F32),
+            V((4, 112, 128), F32),
+            V((5, 16, 8, HALF), F32),
+            V((10, 8, HALF), F32),
+            V((10, 8, HALF), F32),
+            V((8, 128), F32),
+            V((16, 8, 128), F32),
+            dma((5,)),
+            dma((2,)),
+            pltpu.SemaphoreType.REGULAR,
+            dma((3,)),
+            dma((5, 2)),
+            dma((5, 2)),
+            dma((6,)),
+            dma((6,)),
+            dma((5,)),
+            dma((5, 4)),
+            dma((5,)),
+            dma((5, 4)),
+            dma((5,)),
+            dma((5,)),
+            dma((5,)),
+            dma((5,)),
+            dma,
+            dma((5,)),
+            dma((4,)),
+            dma((4,)),
+            dma((4,)),
+            dma((4,)),
+            dma,
+            dma((6,)),
+            dma,
+            dma,
+        ],
+        compiler_params=pltpu.CompilerParams(
+            collective_id=1, has_side_effects=True, vmem_limit_bytes=63 << 20
+        ),
+        cost_estimate=pl.CostEstimate(flops=46 * 10**9, bytes_accessed=60 * 10**6, transcendentals=0),
+    )(lens, norm, rs, perm, w, wmn, wmw, h, xh, y, nar, wid, cot)
+
+
+def prepare(lengths, norm_params):
+    x = lax.axis_index("batch")
+    mine = jnp.broadcast_to(lengths.astype(F32)[:, None], (4, HALF))
+    lens = jnp.zeros((8, HALF), F32)
+    lens = lax.dynamic_update_slice(lens, mine, (4 * x, 0))
+    half = lax.dynamic_slice(norm_params, (0, 0, x * HALF), (2, 10, HALF))
+    norm = jnp.pad(jnp.transpose(half, (1, 0, 2)), ((0, 0), (0, 6), (0, 0)))
+    places = np.arange(384)
+    perm = np.zeros((384, 512), np.float32)
+    perm[places, (places // 24) * 32 + places % 24] = 1.0
+    return lens, norm, jnp.asarray(perm, BF)
+
+
+def body_split(
+    source_narrow,
+    source_wide,
+    lengths,
+    cotangent,
+    kernel_first,
+    kernel_rest,
+    mixer_narrow,
+    mixer_wide,
+    norm_params,
+    moment_first,
+    square_first,
+    moment_rest,
+    square_rest,
+    moment_narrow,
+    square_narrow,
+    moment_wide,
+    square_wide,
+    moment_norm,
+    square_norm,
+):
+    lens, norm, perm = prepare(lengths, norm_params)
+    w, wmn, wmw, h, xh, y, nar, wid, cot, rs, lens = run_forward(
+        lens,
+        norm,
+        perm,
+        source_narrow,
+        source_wide,
+        cotangent,
+        kernel_first,
+        kernel_rest,
+        mixer_narrow,
+        mixer_wide,
+    )
+    mixed, gn, gw, gf, gr, gmn, gmw, ng, total = run_backward(
+        lens, norm, rs, perm, w, wmn, wmw, h, xh, y, nar, wid, cot
+    )
+    grad_norm = jnp.sqrt(total[0, 0])
+    clip = jnp.minimum(1.0, THRESHOLD / grad_norm)
+    norm_grad = jnp.transpose(ng[:, :, :2, :], (2, 1, 0, 3)).reshape(2, 10, CO)
+    results = []
+    for p, g, m, v in (
+        (kernel_first, gf, moment_first, square_first),
+        (kernel_rest, gr, moment_rest, square_rest),
+        (mixer_narrow, gmn, moment_narrow, square_narrow),
+        (mixer_wide, gmw, moment_wide, square_wide),
+    ):
+        results += adamw(p, clip * g, m, v, RATE_WEIGHT, DECAY)
+    results += adamw(norm_params, clip * norm_grad, moment_norm, square_norm, RATE_NORM, 0.0)
+    return (mixed, gn, gw, grad_norm, *results)
+
+
 def solution(mesh):
     in_specs = (
         P(None, "batch", "tm", None),
@@ -340,4 +1978,6 @@
         P(),
         P(),
     )
-    return jax.shard_map(body, mesh=mesh, in_specs=in_specs, out_specs=out_specs, check_vma=False)
+    fits = mesh.shape["tm"] == 16 and mesh.shape["batch"] == 2
+    chosen = body_split if fits else body
+    return jax.shard_map(chosen, mesh=mesh, in_specs=in_specs, out_specs=out_specs, check_vma=False)

time: 2440 us -> 524 us (0.21)
  waiting for transfers between devices: 800 us -> 0 us
  blocking collectives: 751 us -> 0 us
  Pallas kernels: 0 us -> 488 us
  local copies, waits for them, and re-layouts: 393 us -> 5.78 us
  matrix products: 281 us -> 0 us
  other arithmetic: 141 us -> 20.5 us
  starting transfers between devices: 31.4 us -> 0 us
    psum x17 -> x0, blocking collectives: 698 us -> none  [the longest x6 245 us: batch_statistics(): got = lax.psum(sums + extra, ('tm', 'batch'))]
    reduce_scatter x4 -> x0, waiting for transfers between devices: 634 us -> none  [the longest x1 634 us: body(): lax.psum_scatter(shard_gradients[1], 'tm', scatter_dimension=1, tiled=True)]
    pallas_call x0 -> x2, Pallas kernels: none -> 488 us  [the longest x1 260 us: run_backward(): pl.pallas_call(backward_kernel, out_shape=(S((4, 128, 512), BF), S((3, 4,...]
    another operation x19 -> x0, local copies, waits for them, and re-layouts: 329 us -> none  [the longest x5 145 us: body(): jnp.stack(tap_grads, axis=1).reshape(padded.shape[2] * K, CO)]
    dot_general x270 -> x0, matrix products: 281 us -> none  [the longest x85 108 us: body(): jnp.einsum('btd,cd->btc', grad_padded[:, start:start + frames], kernels[i...]
    psum x2 -> x0, waiting for transfers between devices: 80.1 us -> none  [the longest x1 75.9 us: body(): lax.psum(shards[0].astype(jnp.bfloat16), 'batch').astype(jnp.float32)]
    all_gather x2 -> x0, waiting for transfers between devices: 79.8 us -> none  [the longest x1 69 us: body(): lax.all_gather(kernel_rest.astype(jnp.bfloat16), 'tm', axis=1, tiled=True)]
    another operation x5 -> x0, other arithmetic: 53.6 us -> none  [the longest x1 47.1 us: body(): jnp.stack(kernel_grads[1:])]
  transfers between devices with their start and end apart: 28 -> 0, of which waited for: 7 -> 0; matrix products, arithmetic and copies ran while one was open for 28% -> 0% of each run, Pallas kernels for 0% -> 0%
where the time goes in v1:
time: 524 us; the launch traced here: 517 us
  Pallas kernels  488 us (93%)
  other arithmetic  20.5 us (4%)
  local copies, waits for them, and re-layouts  5.78 us (1%)
    pallas_call x1, Pallas kernels, run_backward(): pl.pallas_call(backward_kernel, out_shape=(S((4, 128, 512), BF), S((3, 4,...  260 us
    pallas_call x1, Pallas kernels, run_forward(): pl.pallas_call(forward_kernel, out_shape=(S((85, 16, 32, HALF), BF), S((3...  228 us
    sub x5, other arithmetic, adamw(): return (param - rate * (update + decay * param), first_new, second_new)  18.7 us

profile of v1, /device:TPU:0, one launch (start us, length us, event | category | flops | bytes accessed | tf_op | source)
XLA Modules:
  0.0 517.2 jit_solution(16604375259362205673)
XLA Ops:
  0.7 0.7 convert_element_type.5
  1.3 0.1 broadcast_dynamic-update-slice_fusion.lens_in
  1.4 0.7 dynamic-slice_bitcast_fusion
  2.1 0.6 pad.4.norm
  2.8 0.0 copy-done.7
  2.8 227.9 %shard_map.339 = (bf16[85,16,32,256]{3,2,1,0:T(8,128)(2,1)}, bf16[3,256,256]{2,1,0:T(8,128)(2,1)}, bf16[2,512,256]{2,1,0:T(8,128)(2,1)}, bf16[5,2,1024,256]{3,2,...) custom-call(f32[8,256]{1,0:T(8,128)} %copy-done.7, ...), custom_call_target="tpu_custom_call" | custom-call | flops 24000000000 | bytes 60000000 | tf_op jit(solution)/shard_map/pallas_call | solution.py:949
  230.7 0.0 copy-start.6
  230.8 0.0 copy-start.5
  230.8 0.0 copy-start.3
  230.8 260.2 %shard_map.340 = (bf16[4,128,512]{2,1,0:T(8,128)(2,1)}, f32[3,4,128,256]{3,2,1,0:T(8,128)}, f32[2,4,128,384]{3,2,1,0:T(8,128)}, f32[408,512]{1,0:T(8,128)}, f32[...) custom-call(f32[8,256]{1,0:T(8,128)} %get-tuple-element.39.lens_in, ...), custom_call_target="tpu_custom_call" | custom-call | flops 46000001024 | bytes 60000000 | tf_op jit(solution)/shard_map/pallas_call | solution.py:1784
  491.0 1.2 slice.6
  492.9 0.0 copy-start
  492.9 1.1 multiply_bitcast_fusion
  494.0 0.0 copy-done.6
  494.0 1.9 multiply_subtract_fusion.4
  495.9 1.7 multiply_subtract_fusion.2
  497.6 1.8 multiply_subtract_fusion.3
  499.4 3.6 multiply_subtract_fusion.1
  503.0 0.0 copy-done
  503.0 9.8 %multiply_subtract_fusion = (f32[4,544,512]{2,1,0:T(8,128)}, f32[4,544,512]{2,1,0:T(8,128)}, f32[4,544,512]{2,1,0:T(8,128)}) fusion(f32[4,544,512]{2,1,0:T(8,128)} %kr.1, f32[4,544,512]{2,1,0:T(8,128)S(1)} %copy-done, f32[]{:T(128)S(6)} %min_shard_map.3, f32[4,544,512]{2,1,0:T(8,128)} %param.31, f32[4,544,512]{2,1,0:T(8,128)} %param.32), kind=kLoop, calls=%fused_computation.2 | loop fusion | flops 17825792 | bytes 31195140 | tf_op jit(solution)/shard_map/sub | solution.py:44
  512.8 0.0 copy-done.4
  512.8 0.8 copy.45
  513.6 1.1 copy.46
  514.7 1.1 copy.47
  (10 shorter events, 0.0 us)
Async XLA Ops:
  1.4 1.4 copy-start.7
  230.7 263.3 %copy-start.6 = (f32[2,10,512]{2,0,1:T(2,128)S(1)}, f32[2,10,512]{2,0,1:T(2,128)}, u32[]{:S(2)}) copy-start(f32[2,10,512]{2,0,1:T(2,128)} %param.28) | copy-start | bytes 122884
  230.8 265.1 %copy-start.5 = (f32[2,24,512]{2,1,0:T(8,128)S(1)}, f32[2,24,512]{2,1,0:T(8,128)}, u32[]{:S(2)}) copy-start(f32[2,24,512]{2,1,0:T(8,128)} %mw.1) | copy-start | bytes 294916
  230.8 268.6 %copy-start.3 = (f32[408,512]{1,0:T(8,128)S(1)}, f32[408,512]{1,0:T(8,128)}, u32[]{:S(2)}) copy-start(f32[408,512]{1,0:T(8,128)} %kf.1) | copy-start | bytes 2506756
  492.9 10.1 %copy-start = (f32[4,544,512]{2,1,0:T(8,128)S(1)}, f32[4,544,512]{2,1,0:T(8,128)}, u32[]{:S(2)}) copy-start(f32[4,544,512]{2,1,0:T(8,128)} %get-tuple-element.55) | copy-start | bytes 13369348
  503.0 9.8 %copy-start.4 = (bf16[4,128,512]{2,1,0:T(8,128)(2,1)S(1)}, bf16[4,128,512]{2,1,0:T(8,128)(2,1)}, u32[]{:S(2)}) copy-start(bf16[4,128,512]{2,1,0:T(8,128)(2,1)} %get-tuple-element.93) | copy-start | bytes 1572868
  503.0 10.6 %copy-start.2 = (f32[3,4,128,256]{3,2,1,0:T(8,128)S(1)}, f32[3,4,128,256]{3,2,1,0:T(8,128)}, u32[]{:S(2)}) copy-start(f32[3,4,128,256]{3,2,1,0:T(8,128)} %get-tuple-element.94) | copy-start | bytes 4718596
  512.8 2.0 copy-start.1

commit v2 on v1

--- a/solution.py
+++ b/solution.py
@@ -352,9 +352,11 @@
     return (frames.astype(F32) < lens[None]).astype(F32)
 
 
-def share(box, at, t, x, send, recv):
+def share(box, at, rows, t, x, send, recv):
+    mine = box.at[at, t, pl.ds(0, rows)]
+
     def one(d, _):
-        remote(box.at[at, t], box.at[at, t], send, recv, (lax.rem(t + d, 16), x))
+        remote(mine, mine, send, recv, (lax.rem(t + d, 16), x))
         return 0
 
     lax.fori_loop(1, 16, one, 0)
@@ -452,6 +454,7 @@
     def _():
         hA[:, :, pl.ds(1088, HALO), :] = jnp.zeros((5, 2, HALO, HALF), BF)
 
+    st[...] = jnp.zeros((7, 16, 8, HALF), F32)
     lenr[0] = lens_in[...]
     greet(x, t)
 
@@ -465,88 +468,69 @@
                 v = pf[layer, b, pl.ds(k, count, stride=17), :]
                 if count < 32:
                     v = jnp.concatenate([v, jnp.zeros((32 - count, 128), F32)], axis=0)
-                W[17 * layer + k, t, :, pl.ds(128 * b, 128)] = v.astype(BF)
-
-    def chunk(g, slot):
-        return W.at[
-            pl.ds(5 * lax.div(g, 2), 5), slot, pl.ds(pl.multiple_of(16 * lax.rem(g, 2), 16), 16)
-        ]
-
-    def amount(g, n):
-        return W.at[
-            pl.ds(5 * lax.div(g, 2), 5),
-            pl.ds(0, n),
-            pl.ds(pl.multiple_of(16 * lax.rem(g, 2), 16), 16),
-        ]
-
-    def along(dz):
-        return lax.rem(zi + dz, 4) * 4 + yi * 2 + ci
-
-    def own_sends(block, send, into_z, into_y, into_c):
-        mine = block(t)
+                W[17 * layer + k, zi, yi, ci, :, pl.ds(128 * b, 128)] = v.astype(BF)
+
+    def taps(g):
+        return pl.ds(5 * lax.div(g, 2), 5)
+
+    def part(g):
+        return pl.ds(pl.multiple_of(16 * lax.rem(g, 2), 16), 16)
+
+    def first_sends(own, send, into_z):
         for dz in (1, 2, 3):
-            remote(mine, mine, send, into_z, (along(dz), x))
-        remote(mine, mine, send, into_y, across)
-        remote(mine, mine, send, into_c, sibling)
-
-    def pass_z(block, send, into_y, into_c):
-        for dz in (1, 2, 3):
-            got = block(along(dz))
-            remote(got, got, send, into_y, across)
-            remote(got, got, send, into_c, sibling)
-
-    def pass_y(block, send, into_c):
-        for zz in range(4):
-            got = block(zz * 4 + (1 - yi) * 2 + ci)
-            remote(got, got, send, into_c, sibling)
+            remote(own, own, send, into_z, (lax.rem(zi + dz, 4) * 4 + yi * 2 + ci, x))
+
+    def pass_z(line, send, into_y, into_c):
+        remote(line, line, send, into_y, across)
+        remote(line, line, send, into_c, sibling)
 
     def service(g):
         @pl.when(g < GROUPS)
         def _():
-            own_sends(lambda s: chunk(g, s), ag_s.at[g], rz.at[g], ry.at[g], rc.at[g])
-
-        @pl.when((g >= 1) & (g <= GROUPS))
-        def _():
-            h = g - 1
-            wait_on(amount(h, 3), rz.at[h])
-            pass_z(lambda s: chunk(h, s), ag_s.at[h], ry.at[h], rc.at[h])
+            first_sends(W.at[taps(g), zi, yi, ci, part(g)], ag_s.at[g], rz.at[g])
 
         @pl.when((g >= 2) & (g <= GROUPS + 1))
         def _():
             h = g - 2
-            wait_on(amount(h, 4), ry.at[h])
-            pass_y(lambda s: chunk(h, s), ag_s.at[h], rc.at[h])
-
-        @pl.when((g >= 3) & (g <= GROUPS + 2))
-        def _():
-            h = g - 3
-            wait_on(amount(h, 8), rc.at[h])
-
-        mixer = lambda s: G.at[s]
+            wait_on(W.at[taps(h), pl.ds(0, 3), 0, 0, part(h)], rz.at[h])
+            pass_z(W.at[taps(h), :, yi, ci, part(h)], ag_s.at[h], ry.at[h], rc.at[h])
+
+        @pl.when((g >= 4) & (g <= GROUPS + 3))
+        def _():
+            h = g - 4
+            line = W.at[taps(h), :, 1 - yi, ci, part(h)]
+            wait_on(line, ry.at[h])
+            remote(line, line, ag_s.at[h], rc.at[h], sibling)
+
+        @pl.when((g >= 5) & (g <= GROUPS + 4))
+        def _():
+            h = g - 5
+            wait_on(W.at[taps(h), :, :, 0, part(h)], rc.at[h])
 
         @pl.when(g == 8)
         def _():
-            own_sends(mixer, m_s, m_r.at[0], m_r.at[1], m_r.at[2])
-
-        @pl.when(g == 9)
-        def _():
-            wait_on(G.at[pl.ds(0, 3)], m_r.at[0])
-            pass_z(mixer, m_s, m_r.at[1], m_r.at[2])
+            first_sends(G.at[zi, yi, ci], m_s, m_r.at[0])
 
         @pl.when(g == 10)
         def _():
-            wait_on(G.at[pl.ds(0, 4)], m_r.at[1])
-            pass_y(mixer, m_s, m_r.at[2])
-
-        @pl.when(g == 11)
-        def _():
-            wait_on(G.at[pl.ds(0, 8)], m_r.at[2])
-            for j in range(3):
-                for s in range(16):
-                    wmn[j, pl.ds(16 * s, 16), :] = G[s, pl.ds(16 * j, 16), :]
-            for j in range(2):
-                for s in range(16):
-                    wmw[j, pl.ds(32 * s, 32), :] = G[s, pl.ds(48 + 32 * j, 32), :]
+            wait_on(G.at[pl.ds(0, 3), 0, 0], m_r.at[0])
+            pass_z(G.at[:, yi, ci], m_s, m_r.at[1], m_r.at[2])
+
+        @pl.when(g == 12)
+        def _():
+            line = G.at[:, 1 - yi, ci]
+            wait_on(line, m_r.at[1])
+            remote(line, line, m_s, m_r.at[2], sibling)
+
+        @pl.when(g == 13)
+        def _():
+            wait_on(G.at[:, :, 0], m_r.at[2])
+            for s in range(16):
+                got = G.at[s // 4, s // 2 % 2, s % 2]
+                for j in range(3):
+                    wmn[j, pl.ds(16 * s, 16), :] = got[pl.ds(16 * j, 16), :]
+                for j in range(2):
+                    wmw[j, pl.ds(32 * s, 32), :] = got[pl.ds(48 + 32 * j, 32), :]
 
     def serve(first, last):
         def one(g, _):
@@ -565,9 +549,9 @@
     for layer in (2, 3, 4):
         prep(layer, 32)
     for j in range(3):
-        G[t, pl.ds(16 * j, 16), :] = pmn[j].astype(BF)
+        G[zi, yi, ci, pl.ds(16 * j, 16), :] = pmn[j].astype(BF)
     for j in range(2):
-        G[t, pl.ds(48 + 32 * j, 32), :] = jnp.concatenate(
+        G[zi, yi, ci, pl.ds(48 + 32 * j, 32), :] = jnp.concatenate(
             [pmw[j], jnp.zeros((8, HALF), F32)], axis=0
         ).astype(BF)
     serve(1, 3)
@@ -617,16 +601,15 @@
             (t - 1 + 2 * side, x if to is None else jnp.where(to == 0, x, 1 - x)),
         )
 
-    def halo_wait(layer, send):
-        @pl.when(t > 0)
-        def _():
-            for h in range(2):
-                wait_on(hA.at[layer, h, pl.ds(0, HALO)], (halo_s if send else halo_r).at[layer, 0 if send else 1, h])
-
-        @pl.when(t < 15)
-        def _():
-            for h in range(2):
-                wait_on(hA.at[layer, h, pl.ds(0, HALO)], (halo_s if send else halo_r).at[layer, 1 if send else 0, h])
+    def halo_wait(layer, half, sems, sides):
+        for side, edge in sides:
+
+            @pl.when(t != edge)
+            def _():
+                wait_on(hA.at[layer, half, pl.ds(0, HALO)], sems.at[layer, side, half])
+
+    ARRIVE = ((1, 0), (0, 15))
+    DEPART = ((0, 0), (1, 15))
 
     @pl.when(t > 0)
     def _():
@@ -640,19 +623,16 @@
 
     remote(src_n, rawn.at[x], xr_s.at[2], xr_r.at[2], partner)
     remote(src_w.at[0], raww.at[x, 0], xr_s.at[3], xr_r.at[3], partner)
-    serve(3, 11)
-
-    def shift_copy(layer):
+    serve(3, 13)
+
+    def shift_copy(layer, half):
         def one(b, _):
-            for h in range(2):
-                v = hA[layer, h, pl.ds(pl.multiple_of(b * 128, 128), 144), :].astype(F32)
-                hB[h, pl.ds(pl.multiple_of(b * 128, 128), 128), :] = v[8:136].astype(BF)
+            v = hA[layer, half, pl.ds(pl.multiple_of(b * 128, 128), 144), :].astype(F32)
+            hB[half, pl.ds(pl.multiple_of(b * 128, 128), 128), :] = v[8:136].astype(BF)
             return 0
 
         lax.fori_loop(0, 9, one, 0)
 
-    halo_wait(0, False)
-    shift_copy(0)
 
     def rows_of(b):
         return pl.ds(pl.multiple_of(b * 128, 128), 128)
@@ -678,84 +658,100 @@
         )
         return mean, m2
 
+    def put_stats(ref, layer, field):
+        mean, m2 = local_stats(ref)
+        st[layer, t, pl.ds(2 * field, 1), :] = mean
+        st[layer, t, pl.ds(2 * field + 1, 1), :] = m2
+
+    def combine(at):
+        zero = jnp.zeros((8, HALF), F32)
+        count = lax.fori_loop(0, 16, lambda s, a: a + nv[s], zero)
+        mean = lax.fori_loop(0, 16, lambda s, a: a + nv[s] * st[at, s], zero) / count
+
+        def gather_spread(s, a):
+            v = st[at, s]
+            d = v - mean
+            return a[0] + nv[s] * d * d, a[1] + v
+
+        between, inside = lax.fori_loop(0, 16, gather_spread, (zero, zero))
+
+        def moments(field):
+            m = mean[2 * field : 2 * field + 1]
+            q = inside[2 * field + 1 : 2 * field + 2] + between[2 * field : 2 * field + 1]
+            return m, lax.rsqrt(q / count[:1] + EPS)
+
+        return moments
+
+    def branch_fields(at, number, inputs):
+        for j in range(number):
+            total = None
+            for lhs, rhs in inputs(j):
+                v = jnp.dot(lhs, rhs, preferred_element_type=F32)
+                total = v if total is None else total + v
+            zb[j] = total
+            put_stats(zb.at[j], at, j)
+        share(st, at, 8, t, x, st_s.at[at], st_r.at[at])
+
+    def taps_of(layer, half, lo, rows):
+        for k in range(17):
+            lhs = (
+                hA[layer, half, pl.ds(lo + 8 * k, rows), :]
+                if k % 2 == 0
+                else hB[half, pl.ds(lo + 8 * (k - 1), rows), :]
+            )
+            rhs = W[17 * layer + k, pl.ds(2 * half, 2)].reshape(HALF, HALF)
+            yield jnp.dot(lhs, rhs, preferred_element_type=F32)
+
+    PIECES = ((64, 320), (384, 256), (640, 256), (896, 192))
+
     def layer_step(layer, _):
+        base = 13 + 7 * layer
+        service(base)
         pltpu.make_async_copy(
             W.at[pl.ds(17 * layer, 17)], w_out.at[pl.ds(17 * layer, 17)], out_s.at[layer]
         ).start()
+
+        halo_wait(layer, x, halo_r, ARRIVE)
+        shift_copy(layer, x)
+        acc = jnp.zeros((ROWS, HALF), F32)
+        for v in taps_of(layer, x, 0, ROWS):
+            acc = acc + v
+        z[...] = acc
+        service(base + 1)
+
+        halo_wait(layer, 1 - x, halo_r, ARRIVE)
+        for j, (lo, rows) in enumerate(PIECES):
+
+            @pl.when(layer > 0)
+            def _():
+                wait_on(hA.at[layer, 1 - x, pl.ds(lo, rows)], x_r.at[layer, j])
+
+            a = 0 if j == 0 else 256 * j + 112
+            n = 368 if j == 0 else 256
+            v = hA[layer, 1 - x, pl.ds(a, n + 16), :].astype(F32)
+            hB[1 - x, pl.ds(a, n), :] = v[8 : n + 8].astype(BF)
+            acc = z[pl.ds(256 * j, 256), :]
+            for v in taps_of(layer, 1 - x, 256 * j, 256):
+                acc = acc + v
+            z[pl.ds(256 * j, 256), :] = acc
+            if j == 1:
+                service(base + 2)
+
         pltpu.make_async_copy(
             hA.at[layer, :, pl.ds(HALO, ROWS)], h_out.at[layer], out_s.at[5 + layer]
         ).start()
-
-        acc = jnp.zeros((ROWS, HALF), F32)
-        for k in range(17):
-            for h in range(2):
-                lhs = (
-                    hA[layer, h, pl.ds(8 * k, ROWS), :]
-                    if k % 2 == 0
-                    else hB[h, pl.ds(8 * (k - 1), ROWS), :]
-                )
-                acc = acc + jnp.dot(
-                    lhs,
-                    W[17 * layer + k, pl.ds(8 * h, 8)].reshape(HALF, HALF),
-                    preferred_element_type=F32,
-                )
-        z[...] = acc
-
-        @pl.when(layer == 1)
-        def _():
-            for j in range(3):
-                zb[j] = jnp.dot(nar[j], wmn[j], preferred_element_type=F32)
-
-        @pl.when(layer == 2)
-        def _():
-            zb[0] = jnp.dot(
-                wid[0], wmw[0, pl.ds(0, HALF), :], preferred_element_type=F32
-            ) + jnp.dot(wid[1], wmw[0, pl.ds(HALF, HALF), :], preferred_element_type=F32)
-            zb[1] = jnp.dot(
-                hA[0, 0, pl.ds(HALO, ROWS), :],
-                wmw[1, pl.ds(0, HALF), :],
-                preferred_element_type=F32,
-            ) + jnp.dot(
-                hA[0, 1, pl.ds(HALO, ROWS), :],
-                wmw[1, pl.ds(HALF, HALF), :],
-                preferred_element_type=F32,
-            )
-
-        def put_stats(ref, field):
-            mean, m2 = local_stats(ref)
-            st[layer, t, pl.ds(2 * field, 1), :] = mean
-            st[layer, t, pl.ds(2 * field + 1, 1), :] = m2
-
-        st[layer, t] = jnp.zeros((8, HALF), F32)
-        put_stats(z, 0)
-        for at, number in ((1, 3), (2, 2)):
-
-            @pl.when(layer == at)
-            def _():
-                for j in range(number):
-                    put_stats(zb.at[j], 1 + j)
-
-        share(st, layer, t, x, st_s.at[layer], st_r.at[layer])
-        wait_on(st.at[layer, pl.ds(0, 15)], st_r.at[layer])
-        zero = jnp.zeros((8, HALF), F32)
-        count = lax.fori_loop(0, 16, lambda s, a: a + nv[s], zero)
-        mean = lax.fori_loop(0, 16, lambda s, a: a + nv[s] * st[layer, s], zero) / count
-
-        def gather_spread(s, a):
-            v = st[layer, s]
-            d = v - mean
-            return a[0] + nv[s] * d * d, a[1] + v
-
-        between, inside = lax.fori_loop(0, 16, gather_spread, (zero, zero))
-
-        def moments(field):
-            m = mean[2 * field : 2 * field + 1]
-            q = (inside[2 * field + 1 : 2 * field + 2] + between[2 * field : 2 * field + 1]) / count[:1]
-            return m, lax.rsqrt(q + EPS)
-
-        def branches(base, number):
+        put_stats(z, layer, 0)
+        share(st, layer, 2, t, x, st_s.at[layer], st_r.at[layer])
+        service(base + 3)
+        service(base + 4)
+        wait_on(st.at[layer, pl.ds(0, 15), pl.ds(0, 2)], st_r.at[layer])
+        moments = combine(layer)
+
+        def branches(at, base, number):
+            wait_on(st.at[at, pl.ds(0, 15)], st_r.at[at])
+            shares = combine(at)
             for j in range(number):
-                m, r = moments(1 + j)
+                m, r = shares(j)
                 field = base + j
                 rs_out[field] = jnp.broadcast_to(r, (8, HALF))
                 gain = norm[field, pl.ds(0, 1), :]
@@ -788,45 +784,38 @@
         @pl.when(layer < 4)
         def _():
             def one(b, _):
-                v = (z[rows_of(b), :] - m) * r
-                xhb[0, rows_of(b), :] = v
+                rows = pl.ds(pl.multiple_of(b * 64, 64), 64)
+                v = (z[rows, :] - m) * r
+                xhb[0, rows, :] = v
                 y = gain * v + bias
-                a = (y * jax.nn.sigmoid(y)).reshape(16, 8, HALF) * frame_mask(b, t, lens[...])
-                hA[layer + 1, x, pl.ds(pl.multiple_of(HALO + b * 128, 64), 128), :] = a.reshape(
-                    128, HALF
+                frames = lax.broadcasted_iota(jnp.int32, (8, 8, HALF), 0) + (b * 8 + t * 128)
+                a = (y * jax.nn.sigmoid(y)).reshape(8, 8, HALF)
+                a = jnp.where(frames.astype(F32) < lens[...][None], a, 0.0)
+                hA[layer + 1, x, pl.ds(pl.multiple_of(HALO + b * 64, 64), 64), :] = a.reshape(
+                    64, HALF
                 ).astype(BF)
                 return 0
 
-            lax.fori_loop(0, 8, one, 0)
-
-            @pl.when(t > 0)
-            def _():
-                for to in range(2):
-                    a = hA.at[layer + 1, x, pl.ds(HALO, HALO)]
-                    b = hA.at[layer + 1, x, pl.ds(1088, HALO)]
-                    remote(
-                        a,
-                        b,
-                        halo_s.at[layer + 1, 0, to],
-                        halo_r.at[layer + 1, 0, x],
-                        (t - 1, x if to == 0 else 1 - x),
-                    )
-
-            @pl.when(t < 15)
-            def _():
-                for to in range(2):
-                    a = hA.at[layer + 1, x, pl.ds(1024, HALO)]
-                    b = hA.at[layer + 1, x, pl.ds(0, HALO)]
-                    remote(
-                        a,
-                        b,
-                        halo_s.at[layer + 1, 1, to],
-                        halo_r.at[layer + 1, 1, x],
-                        (t + 1, x if to == 0 else 1 - x),
-                    )
-
-            inner = hA.at[layer + 1, x, pl.ds(HALO, ROWS)]
-            remote(inner, inner, x_s.at[layer], x_r.at[layer], partner)
+            done = 0
+            for j, (lo, rows) in enumerate(PIECES):
+                last = (lo + rows - HALO) // 64
+                lax.fori_loop(done, last, one, 0)
+                done = last
+                ref = hA.at[layer + 1, x, pl.ds(lo, rows)]
+                remote(ref, ref, x_s.at[layer + 1, j], x_r.at[layer + 1, j], partner)
+            for side, edge in DEPART:
+
+                @pl.when(t != edge)
+                def _():
+                    lo, to = ((HALO, 1088), (1024, 0))[side]
+                    for other in range(2):
+                        remote(
+                            hA.at[layer + 1, x, pl.ds(lo, HALO)],
+                            hA.at[layer + 1, x, pl.ds(to, HALO)],
+                            halo_s.at[layer + 1, side, other],
+                            halo_r.at[layer + 1, side, x],
+                            (t - 1 + 2 * side, x if other == 0 else 1 - x),
+                        )
 
         @pl.when(layer == 4)
         def _():
@@ -840,9 +829,7 @@
 
         pltpu.make_async_copy(xhb.at[0], xh_out.at[layer], out_s.at[11]).start()
 
-        @pl.when(layer < 4)
-        def _():
-            serve(11 + 7 * layer, 18 + 7 * layer)
+        service(base + 5)
 
         @pl.when(layer == 0)
         def _():
@@ -857,10 +844,13 @@
                     return 0
 
                 lax.fori_loop(0, 8, one, 0)
+                if j == 0:
+                    service(base + 6)
 
         @pl.when(layer == 1)
         def _():
-            branches(5, 3)
+            branches(5, 5, 3)
+            service(base + 6)
             wait_on(raww.at[0, 0], xr_r.at[3])
             spread_wide(0)
 
@@ -873,12 +863,14 @@
 
         @pl.when(layer == 2)
         def _():
-            branches(8, 2)
+            branches(6, 8, 2)
+            service(base + 6)
             copies[14].wait()
             remote(cot.at[:, :, other], rawc.at[x], xr_s.at[4], xr_r.at[4], partner)
 
         @pl.when(layer == 3)
         def _():
+            service(base + 6)
             wait_on(rawc.at[0], xr_r.at[4])
             for s in range(8):
                 spread_half(rawc[s // 4, s % 4], s)
@@ -889,11 +881,19 @@
 
             lax.fori_loop(0, 8, one, 0)
 
-        @pl.when(layer < 4)
-        def _():
-            wait_on(hA.at[0, 0, pl.ds(HALO, ROWS)], x_r.at[layer])
-            halo_wait(layer + 1, False)
-            shift_copy(layer + 1)
+
+        @pl.when(layer == 0)
+        def _():
+            branch_fields(5, 3, lambda j: [(nar[j], wmn[j])])
+
+        @pl.when(layer == 1)
+        def _():
+            def inputs(j):
+                for h in range(2):
+                    lhs = wid[h] if j == 0 else hA[0, h, pl.ds(HALO, ROWS), :]
+                    yield lhs, wmw[j, pl.ds(HALF * h, HALF), :]
+
+            branch_fields(6, 2, inputs)
 
         return 0
 
@@ -917,11 +917,11 @@
         wait_on(hA.at[0, :, pl.ds(HALO, ROWS)], out_s.at[5 + i])
 
     def drained(g, _):
-        wait_on(amount(g, 15), ag_s.at[g])
+        wait_on(W.at[pl.ds(0, 75), 0, 0, 0, pl.ds(0, 16)], ag_s.at[g])
         return 0
 
     lax.fori_loop(0, GROUPS, drained, 0)
-    wait_on(G.at[pl.ds(0, 15)], m_s)
+    wait_on(W.at[pl.ds(0, 35), pl.ds(0, 3), 0, 0, pl.ds(0, 16)], m_s)
     wait_on(lenr.at[0], xr_s.at[0])
     wait_on(raww.at[0, 1], xr_s.at[1])
     wait_on(rawn.at[0], xr_s.at[2])
@@ -929,16 +929,20 @@
     wait_on(rawc.at[0], xr_s.at[4])
 
     def finish(layer, _):
-        halo_wait(layer, True)
-        wait_on(st.at[layer, pl.ds(0, 15)], st_s.at[layer])
-
-        @pl.when(layer < 4)
-        def _():
-            wait_on(hA.at[0, 0, pl.ds(HALO, ROWS)], x_s.at[layer])
+        for h in range(2):
+            halo_wait(layer, h, halo_s, DEPART)
+        wait_on(st.at[layer, pl.ds(0, 15), pl.ds(0, 2)], st_s.at[layer])
+
+        @pl.when(layer > 0)
+        def _():
+            for j, (lo, rows) in enumerate(PIECES):
+                wait_on(hA.at[0, 0, pl.ds(lo, rows)], x_s.at[layer, j])
 
         return 0
 
     lax.fori_loop(0, 5, finish, 0)
+    for at in (5, 6):
+        wait_on(st.at[at, pl.ds(0, 15)], st_s.at[at])
 
 
 def run_forward(lens, norm, perm, src_n, src_w, cot, kf, kr, mn, mw):
@@ -949,7 +953,7 @@
     return pl.pallas_call(
         forward_kernel,
         out_shape=(
-            S((85, 16, 32, HALF), BF),
+            S((85, 4, 2, 2, 32, HALF), BF),
             S((3, HALF, HALF), BF),
             S((2, 512, HALF), BF),
             S((5, 2, ROWS, HALF), BF),
@@ -964,8 +968,8 @@
         in_specs=[vm, vm, vm] + [hb] * 7,
         out_specs=[hb] * 9 + [vm, vm],
         scratch_shapes=[
-            pltpu.VMEM((85, 16, 32, HALF), BF),
-            pltpu.VMEM((16, 112, HALF), BF),
+            pltpu.VMEM((85, 4, 2, 2, 32, HALF), BF),
+            pltpu.VMEM((4, 2, 2, 112, HALF), BF),
             pltpu.VMEM((3, HALF, HALF), BF),
             pltpu.VMEM((2, 512, HALF), BF),
             pltpu.VMEM((5, 2, 1168, HALF), BF),
@@ -984,7 +988,7 @@
             pltpu.VMEM((3, ROWS, HALF), BF),
             pltpu.VMEM((2, ROWS, HALF), BF),
             pltpu.VMEM((ROWS, HALF), BF),
-            pltpu.VMEM((5, 16, 8, HALF), F32),
+            pltpu.VMEM((7, 16, 8, HALF), F32),
             pltpu.VMEM((16, 8, HALF), F32),
             pltpu.VMEM((2, 8, HALF), F32),
             pltpu.VMEM((8, HALF), F32),
@@ -995,14 +999,14 @@
             dma((GROUPS,)),
             dma,
             dma((3,)),
-            dma((4,)),
-            dma((4,)),
+            dma((5, 4)),
+            dma((5, 4)),
             dma((5,)),
             dma((5,)),
             dma((5, 2, 2)),
             dma((5, 2, 2)),
-            dma((5,)),
-            dma((5,)),
+            dma((7,)),
+            dma((7,)),
             dma((18,)),
         ],
         compiler_params=pltpu.CompilerParams(
@@ -1070,13 +1074,13 @@
     gst,
     gsm,
     bst,
+    sums4,
     ngr,
     ngx,
     ss,
     fst,
     load_s,
     w_s,
-    go,
     br_s,
     halo_s,
     halo_r,
@@ -1144,6 +1148,7 @@
             dzA[:, pl.ds(lo, HALO), :] = jnp.zeros((2, HALO, HALF), BF)
 
     dzA[:, pl.ds(1152, 16), :] = jnp.zeros((2, 16, HALF), BF)
+    bst[...] = jnp.zeros((5, 16, 8, HALF), F32)
     barrier = pltpu.get_barrier_semaphore()
 
     def greet_one(d, _):
@@ -1173,125 +1178,117 @@
                 own(i, b, sequence(b, 4 * x + i))
                 send(i, b, sequence(b, 4 * (1 - x) + i))
 
-    wait_on(y5, load_s.at[3])
-
-    def out_block(b, _):
-        y = y5[rows_of(b), :]
-        a = (y * jax.nn.sigmoid(y)).reshape(16, 8, HALF) * mask(b)
-        a = a.reshape(128, HALF)
-        for i in range(2):
-            stg[i, rows_of(b), :] = a[:, 128 * i : 128 * i + 128]
-        return 0
-
-    lax.fori_loop(0, 8, out_block, 0)
-
     def mix_put(ref):
         def put(i, b, v):
             ref[i, :, pl.ds(128 * b, 128)] = v.astype(BF)
 
         return put
 
-    unstage(2, mix_put(mix_own.at[0]), mix_put(mix_own.at[1]))
-    remote(mix_own.at[1], mix_rcv, sn_s.at[0], sn_r.at[0], partner)
     my_cols = pl.ds(pl.multiple_of(x * HALF, HALF), HALF)
     other_cols = pl.ds(pl.multiple_of((1 - x) * HALF, HALF), HALF)
-    copy_in(mix_own.at[0], mixed_out.at[:, :, my_cols], out_s.at[0])
-
-    wait_on(sb.at[0], load_s.at[4])
-
-    def start_da(b, _):
-        da[rows_of(b), :] = sb[0, rows_of(b), :].astype(F32)
-        return 0
-
-    lax.fori_loop(0, 8, start_da, 0)
-
-    def slot_z(q):
-        return lax.rem(zi + 1 + q, 4)
-
-    def send_core(layer):
+
+    def send_mixed():
+        unstage(2, mix_put(mix_own.at[0]), mix_put(mix_own.at[1]))
+        remote(mix_own.at[1], mix_rcv, sn_s.at[0], sn_r.at[0], partner)
+        copy_in(mix_own.at[0], mixed_out.at[:, :, my_cols], out_s.at[0])
+
+    ORDER = (0, 3, 1, 2)
+
+    def send_core(layer, zs):
         b3, b2 = lax.rem(layer, 3), lax.rem(layer, 2)
-        for q in range(4):
-            zz = slot_z(q)
+        for zz in zs:
             remote(
                 dW.at[b3, :, zz, :, 1 - ci],
                 crecv.at[b2, :, zz],
                 c_s.at[layer],
-                c_r.at[layer, q],
+                c_r.at[layer, zz],
                 sibling,
             )
 
-    def add_core(layer, q):
+    def add_core(layer, u, n=17):
         b3, b2 = lax.rem(layer, 3), lax.rem(layer, 2)
-        zz = slot_z(q)
-        wait_on(crecv.at[b2, :, zz], c_r.at[layer, q])
-        for yy in range(2):
-
-            def one(k, _):
+        zz, lo = ORDER[u // 2], n * (u % 2)
+        if u % 2 == 0:
+            wait_on(crecv.at[b2, :, zz], c_r.at[layer, zz])
+
+        def one(k, _):
+            for yy in range(2):
                 dW[b3, k, zz, yy, ci] = (
                     dW[b3, k, zz, yy, ci].astype(F32) + crecv[b2, k, zz, yy].astype(F32)
                 ).astype(BF)
-                return 0
-
-            lax.fori_loop(0, 17, one, 0)
+            return 0
+
+        lax.fori_loop(lo, lo + n, one, 0)
         remote(
-            dW.at[b3, :, zz, 1 - yi, ci],
-            yrecv.at[b2, :, zz],
+            dW.at[b3, pl.ds(lo, n), zz, 1 - yi, ci],
+            yrecv.at[b3, pl.ds(lo, n), zz],
             y_s.at[layer],
-            y_r.at[layer, q],
+            y_r.at[layer, u],
             across,
         )
 
-    def add_across(layer, q):
-        b3, b2 = lax.rem(layer, 3), lax.rem(layer, 2)
-        zz = slot_z(q)
-        wait_on(yrecv.at[b2, :, zz], y_r.at[layer, q])
+    def add_across(layer, u, n=17):
+        b3 = lax.rem(layer, 3)
+        zz, lo = ORDER[u // 2], n * (u % 2)
+        wait_on(yrecv.at[b3, pl.ds(lo, n), zz], y_r.at[layer, u])
 
         def one(k, _):
             dW[b3, k, zz, yi, ci] = (
-                dW[b3, k, zz, yi, ci].astype(F32) + yrecv[b2, k, zz].astype(F32)
+                dW[b3, k, zz, yi, ci].astype(F32) + yrecv[b3, k, zz].astype(F32)
             ).astype(BF)
             return 0
 
-        lax.fori_loop(0, 17, one, 0)
-        if q < 3:
+        lax.fori_loop(lo, lo + n, one, 0)
+
+        @pl.when(zi != zz)
+        def _():
             remote(
-                dW.at[b3, :, zz, yi, ci],
-                zrecv.at[b2, q],
-                z_s.at[layer],
-                z_r.at[layer],
+                dW.at[b3, pl.ds(lo, n), zz, yi, ci],
+                zrecv.at[b3, lax.rem(zi + 3 - zz, 4), pl.ds(lo, n)],
+                z_s.at[layer, u % 2],
+                z_r.at[layer, u % 2],
                 (zz * 4 + yi * 2 + ci, x),
             )
 
-    def finish_sum(layer):
+    def finish_sum(layer, half, n=17):
         b3, b2 = lax.rem(layer, 3), lax.rem(layer, 2)
-        wait_on(zrecv.at[b2], z_r.at[layer])
-        when(layer + 2 <= 4, lambda: wait_on(fin.at[0], f_s.at[layer + 2]))
+        lo = n * half
+        wait_on(zrecv.at[b3, :, pl.ds(lo, n)], z_r.at[layer, half])
+        if half == 0:
+            when(layer + 2 <= 4, lambda: wait_on(fin.at[0], f_s.at[layer + 2]))
 
         def one(k, _):
             v = dW[b3, k, zi, yi, ci].astype(F32)
             for q in range(3):
-                v = v + zrecv[b2, q, k].astype(F32)
+                v = v + zrecv[b3, q, k].astype(F32)
             fin[b2, k] = v.astype(BF)
             return 0
 
-        lax.fori_loop(0, 17, one, 0)
-        remote(fin.at[b2], xrecv.at[layer], f_s.at[layer], f_r.at[layer], partner)
+        lax.fori_loop(lo, lo + n, one, 0)
+        mine = pl.ds(lo, n)
+        remote(
+            fin.at[b2, mine], xrecv.at[layer, mine], f_s.at[layer], f_r.at[layer, half], partner
+        )
 
     def add_square(v):
         ss[...] += jnp.sum((v * v).reshape(-1, 8, 128), axis=0)
 
-    def assemble(layer, rows, put):
+    def assemble(layer, put, n=17):
         b2 = lax.rem(layer, 2)
-        wait_on(xrecv.at[layer], f_r.at[layer])
-        for k in range(17):
+        rows = 32 if n == 17 else 24
+        for half in range(2):
+            wait_on(xrecv.at[layer, pl.ds(n * half, n)], f_r.at[layer, half])
+        for source, side in ((fin.at[b2], x), (xrecv.at[layer], 1 - x)):
             for b in range(2):
                 lanes = pl.ds(128 * b, 128)
-                gst[2 * x + b, pl.ds(k, rows, stride=17), :] = fin[
-                    b2, k, pl.ds(0, 32), lanes
-                ].astype(F32)[:rows]
-                gst[2 * (1 - x) + b, pl.ds(k, rows, stride=17), :] = xrecv[
-                    layer, k, pl.ds(0, 32), lanes
-                ].astype(F32)[:rows]
+                for k in range(17):
+                    if n == 17:
+                        v = source[pl.ds(2 * k, 2), :, lanes].astype(F32).reshape(32, 128)
+                    else:
+                        lo = 3 * (k // 2) + k % 2
+                        v = source[pl.ds(lo, 2), :, lanes].astype(F32).reshape(32, 128)
+                        v = v[8 * (k % 2) : 8 * (k % 2) + 24]
+                    gst[2 * side + b, pl.ds(k, rows, stride=17), :] = v
         for b in range(4):
             add_square(gst[b, pl.ds(0, rows * 17), :])
             copy_in(gst.at[b, pl.ds(0, rows * 17)], put(b), g_s)
@@ -1299,10 +1296,11 @@
     def wait_assembled(rows):
         wait_on(gst.at[:, pl.ds(0, rows * 17)], g_s)
 
-    def drain_sums(layer):
+    def drain_sums(layer, n=17):
         wait_on(crecv.at[0], c_s.at[layer])
-        wait_on(yrecv.at[0], y_s.at[layer])
-        wait_on(zrecv.at[0], z_s.at[layer])
+        wait_on(yrecv.at[0, pl.ds(0, 2 * n)], y_s.at[layer])
+        for half in range(2):
+            wait_on(zrecv.at[0, :, pl.ds(0, n)], z_s.at[layer, half])
 
     def put_rest(layer):
         return lambda b: gr_out.at[layer - 1, :, pl.ds(128 * b, 128)]
@@ -1322,7 +1320,7 @@
         for zz in range(4):
             Dm[zz, yi, ci] = (Dm[zz, yi, ci].astype(F32) + ym[zz].astype(F32)).astype(BF)
         for q in range(3):
-            zz = slot_z(q)
+            zz = lax.rem(zi + 1 + q, 4)
             remote(Dm.at[zz, yi, ci], zm.at[q], m_s.at[2], m_r.at[2], (zz * 4 + yi * 2 + ci, x))
 
     def mixers_four():
@@ -1361,17 +1359,29 @@
             def _():
                 wait_on(dzA.at[0, pl.ds(0, HALO)], halo_s.at[layer, side])
 
-    def norm_backward(layer, last):
+    def output_gradient(layer, last):
         wait_on(Xl, load_s.at[2])
+        if last:
+            wait_on(y5, load_s.at[3])
+            wait_on(sb.at[0], load_s.at[4])
         gain = norm[layer, pl.ds(0, 1), :]
         bias = norm[layer, pl.ds(1, 1), :]
 
         def one(b, acc):
             xh = Xl[rows_of(b), :]
-            y = y5[rows_of(b), :] if last else gain * xh + bias
+            if last:
+                y = y5[rows_of(b), :]
+                d = sb[0, rows_of(b), :].astype(F32)
+            else:
+                y = gain * xh + bias
+                d = da[rows_of(b), :] + pxr[1 - lax.rem(layer, 2), rows_of(b), :].astype(F32)
             sg = jax.nn.sigmoid(y)
-            v = da[rows_of(b), :] * sg * (1.0 + y * (1.0 - sg))
-            v = v.reshape(16, 8, HALF) * mask(b)
+            m = mask(b)
+            if last:
+                a = ((y * sg).reshape(16, 8, HALF) * m).reshape(128, HALF)
+                for i in range(2):
+                    stg[i, rows_of(b), :] = a[:, 128 * i : 128 * i + 128]
+            v = (d * sg * (1.0 + y * (1.0 - sg))).reshape(16, 8, HALF) * m
             s0 = acc[0] + jnp.sum(v, axis=0)
             s1 = acc[1] + jnp.sum(v * xh.reshape(16, 8, HALF), axis=0)
             v = v.reshape(128, HALF)
@@ -1380,7 +1390,13 @@
                 y5[rows_of(b), :] = v
             return s0, s1
 
-        s0, s1 = lax.fori_loop(0, 8, one, (zero, zero))
+        if last:
+            s0, s1 = lax.fori_loop(0, 8, one, (zero, zero))
+        else:
+            s0, s1 = zero, zero
+            for j in range(4):
+                wait_on(pxr.at[0, pl.ds(0, 256)], px_r.at[layer + 1, j])
+                s0, s1 = lax.fori_loop(2 * j, 2 * j + 2, one, (s0, s1))
         bst[layer, t] = zero
         bst[layer, t, pl.ds(0, 1), :] = jnp.sum(s0, axis=0, keepdims=True)
         bst[layer, t, pl.ds(1, 1), :] = jnp.sum(s1, axis=0, keepdims=True)
@@ -1398,12 +1414,16 @@
 
                 sj = lax.fori_loop(0, 8, branch, zero)
                 bst[layer, t, pl.ds(2 + j, 1), :] = jnp.sum(sj, axis=0, keepdims=True)
-        share(bst, layer, t, x, st_s.at[layer], st_r.at[layer])
-        wait_on(bst.at[layer, pl.ds(0, 15)], st_r.at[layer])
+        share(bst, layer, 8 if last else 2, t, x, st_s.at[layer], st_r.at[layer])
+
+    def field_gradient(layer, last):
+        wait_on(bst.at[layer, pl.ds(0, 15), pl.ds(0, 8 if last else 2)], st_r.at[layer])
+        gain = norm[layer, pl.ds(0, 1), :]
         sums = lax.fori_loop(0, 16, lambda s, a: a + bst[layer, s], zero)
         ngr[layer, pl.ds(0, 1), :] = sums[1:2]
         ngr[layer, pl.ds(1, 1), :] = sums[0:1]
         if last:
+            sums4[...] = sums
             for j in range(5):
                 ngr[5 + j, pl.ds(0, 1), :] = sums[2 + j : 3 + j]
                 ngr[5 + j, pl.ds(1, 1), :] = sums[0:1]
@@ -1436,8 +1456,6 @@
                     (t - 1 + 2 * side, x),
                 )
 
-        return sums
-
     def halo_arrived(layer):
         b2 = lax.rem(layer, 2)
         for side, edge in ((1, 0), (0, 15)):
@@ -1453,221 +1471,272 @@
 
         lax.fori_loop(0, 9, one, 0)
 
-    def shifted(b2, k):
+    def shifted(b2, k, lo=0, rows=ROWS):
         o = 16 - k
         if o % 2 == 0:
-            return dzA[b2, pl.ds(8 * o, ROWS), :]
-        return dzB[pl.ds(8 * (o - 1), ROWS), :]
-
-    def data_half(layer, half):
+            return dzA[b2, pl.ds(8 * o + lo, rows), :]
+        return dzB[pl.ds(8 * (o - 1) + lo, rows), :]
+
+    def data_half(layer, half, lo=0, rows=ROWS):
         b2 = lax.rem(layer, 2)
-        acc = jnp.zeros((ROWS, HALF), F32)
+        acc = jnp.zeros((rows, HALF), F32)
         for k in range(17):
             acc = acc + lax.dot_general(
-                shifted(b2, k),
-                Wl[b2, k, pl.ds(8 * half, 8)].reshape(HALF, HALF),
+                shifted(b2, k, lo, rows),
+                Wl[b2, k, pl.ds(2 * half, 2)].reshape(HALF, HALF),
                 (((1,), (1,)), ((), ())),
                 preferred_element_type=F32,
             )
         return acc
 
-    def weight_gradient(layer):
-        b3, b2 = lax.rem(layer, 3), lax.rem(layer, 2)
-        wait_on(Hl, load_s.at[1])
+    def weight_tap(layer, h, k):
+        return lax.dot_general(
+            Hl[h],
+            shifted(lax.rem(layer, 2), k),
+            (((0,), (0,)), ((), ())),
+            preferred_element_type=F32,
+        ).reshape(2, 2, 2, 32, HALF)
+
+    def weight_gradient(layer, h):
+        b3 = lax.rem(layer, 3)
         for k in range(17):
+            v = weight_tap(layer, h, k)
+            for part in range(2):
+                dW[b3, 2 * k + part, pl.ds(2 * h, 2)] = v[:, :, :, 16 * part : 16 * part + 16].astype(BF)
+
+    def first_weight_gradient(h):
+        for pair in range(9):
+            v = weight_tap(0, h, 2 * pair)[:, :, :, :24]
+            if pair < 8:
+                v = jnp.concatenate([v, weight_tap(0, h, 2 * pair + 1)[:, :, :, :24]], axis=3)
+            else:
+                v = jnp.concatenate([v, jnp.zeros((2, 2, 2, 8, HALF), F32)], axis=3)
+            for part in range(3 if pair < 8 else 2):
+                dW[0, 3 * pair + part, pl.ds(2 * h, 2)] = v[
+                    :, :, :, 16 * part : 16 * part + 16
+                ].astype(BF)
+
+    def load_branch(j):
+        copy_in(xh_in.at[5 + j], xb.at[0], br_s.at[0])
+        if j < 3:
+            copy_in(nar_in.at[j], sb.at[0], br_s.at[2])
+        elif j == 3:
+            copy_in(wid_in, sb, br_s.at[2])
+        else:
+            copy_in(h_in.at[0], sb, br_s.at[2])
+
+    def branch(j):
+        field = 5 + j
+        sums = sums4[...]
+        wait_on(xb.at[0], br_s.at[0])
+        wait_on(sb.at[0] if j < 3 else sb, br_s.at[2])
+        gain = norm[field, pl.ds(0, 1), :]
+        r = rs[field, pl.ds(0, 1), :]
+        c0 = gain * sums[0:1] / count
+        c1 = gain * sums[2 + j : 3 + j] / count
+
+        def one(b, _):
+            m = mask(b)
+            v = (gain * y5[rows_of(b), :]).reshape(16, 8, HALF)
+            xh = xb[0, rows_of(b), :].reshape(16, 8, HALF)
+            v = r * (v - m * c0 - m * xh * c1)
+            px[1, rows_of(b), :] = v.reshape(128, HALF).astype(BF)
+            return 0
+
+        lax.fori_loop(0, 8, one, 0)
+        dv = px[1]
+        if j < 3:
+            v = lax.dot_general(
+                sb[0], dv, (((0,), (0,)), ((), ())), preferred_element_type=F32
+            )
+            Dm[:, :, :, pl.ds(16 * j, 16), :] = v.reshape(4, 2, 2, 16, HALF).astype(BF)
+            back = lax.dot_general(
+                dv, wmn[j], (((1,), (1,)), ((), ())), preferred_element_type=F32
+            )
+            blocks = 2
+        else:
+            i = j - 3
             for h in range(2):
                 v = lax.dot_general(
-                    Hl[h], shifted(b2, k), (((0,), (0,)), ((), ())), preferred_element_type=F32
+                    sb[h], dv, (((0,), (0,)), ((), ())), preferred_element_type=F32
                 )
-                dW[b3, k, pl.ds(2 * h, 2)] = v.reshape(2, 2, 2, 32, HALF).astype(BF)
-
-    def branches(sums):
-        own_first = True
-        for j in range(5):
-            field = 5 + j
-            copy_in(xh_in.at[field], xb.at[0], br_s.at[0])
-            if j < 3:
-                copy_in(nar_in.at[j], sb.at[0], br_s.at[2])
-            elif j == 3:
-                copy_in(wid_in, sb, br_s.at[2])
-            else:
-                copy_in(h_in.at[0], sb, br_s.at[2])
-            wait_on(xb.at[0], br_s.at[0])
-            wait_on(sb.at[0] if j < 3 else sb, br_s.at[2])
-            gain = norm[field, pl.ds(0, 1), :]
-            r = rs[field, pl.ds(0, 1), :]
-            c0 = gain * sums[0:1] / count
-            c1 = gain * sums[2 + j : 3 + j] / count
-
-            def one(b, _):
-                m = mask(b)
-                v = (gain * y5[rows_of(b), :]).reshape(16, 8, HALF)
-                xh = xb[0, rows_of(b), :].reshape(16, 8, HALF)
-                v = r * (v - m * c0 - m * xh * c1)
-                px[1, rows_of(b), :] = v.reshape(128, HALF).astype(BF)
-                return 0
-
-            lax.fori_loop(0, 8, one, 0)
-            dv = px[1]
-            if j < 3:
-                v = lax.dot_general(
-                    sb[0], dv, (((0,), (0,)), ((), ())), preferred_element_type=F32
-                )
-                Dm[:, :, :, pl.ds(16 * j, 16), :] = v.reshape(4, 2, 2, 16, HALF).astype(BF)
-                back = lax.dot_general(
-                    dv, wmn[j], (((1,), (1,)), ((), ())), preferred_element_type=F32
-                )
-                blocks = 2
-            else:
-                i = j - 3
-                for h in range(2):
-                    v = lax.dot_general(
-                        sb[h], dv, (((0,), (0,)), ((), ())), preferred_element_type=F32
-                    )
-                    Dm[pl.ds(2 * h, 2), :, :, pl.ds(48 + 32 * i, 32), :] = v.reshape(
-                        2, 2, 2, 32, HALF
-                    ).astype(BF)
-                wu = jnp.dot(perm[...], wmw[i], preferred_element_type=F32).astype(BF)
-                back = lax.dot_general(
-                    dv, wu, (((1,), (1,)), ((), ())), preferred_element_type=F32
-                )
-                blocks = 3
-            for b in range(blocks):
-                stg[b] = back[:, 128 * b : 128 * b + 128]
-
-            def masked(b, _):
-                m = mask(b)[:, :, :128]
-                for i in range(blocks):
-                    stg[i, rows_of(b), :] = (
-                        stg[i, rows_of(b), :].reshape(16, 8, 128) * m
-                    ).reshape(128, 128)
-                return 0
-
-            lax.fori_loop(0, 8, masked, 0)
-            if j < 3:
-
-                def put_own(i, b, v):
-                    own_n[j, i, :, pl.ds(128 * b, 128)] = v
-
-                def put_send(i, b, v):
-                    snd_n[j, i, :, pl.ds(128 * b, 128)] = v.astype(BF)
-
-            else:
-
-                def put_own(i, b, v):
-                    own_w[j - 3, i, :, pl.ds(128 * b, 128)] = v
-
-                def put_send(i, b, v):
-                    snd_w[j - 3, i, :, pl.ds(128 * b, 128)] = v.astype(BF)
-
-            unstage(blocks, put_own, put_send)
-        remote(snd_n, rcv_n, sn_s.at[1], sn_r.at[1], partner)
-        remote(snd_w.at[pl.ds(0, 2)], rcv_w.at[pl.ds(0, 2)], sn_s.at[2], sn_r.at[2], partner)
+                Dm[pl.ds(2 * h, 2), :, :, pl.ds(48 + 32 * i, 32), :] = v.reshape(
+                    2, 2, 2, 32, HALF
+                ).astype(BF)
+            wu = jnp.dot(perm[...], wmw[i], preferred_element_type=F32).astype(BF)
+            back = lax.dot_general(
+                dv, wu, (((1,), (1,)), ((), ())), preferred_element_type=F32
+            )
+            blocks = 3
+        if j < 4:
+            load_branch(j + 1)
+        for b in range(8):
+            m = mask(b)[:, :, :128]
+            for i in range(blocks):
+                v = back[128 * b : 128 * b + 128, 128 * i : 128 * i + 128]
+                stg[i, pl.ds(128 * b, 128), :] = (v.reshape(16, 8, 128) * m).reshape(128, 128)
+        if j < 3:
+
+            def put_own(i, b, v):
+                own_n[j, i, :, pl.ds(128 * b, 128)] = v
+
+            def put_send(i, b, v):
+                snd_n[j, i, :, pl.ds(128 * b, 128)] = v.astype(BF)
+
+        else:
+
+            def put_own(i, b, v):
+                own_w[j - 3, i, :, pl.ds(128 * b, 128)] = v
+
+            def put_send(i, b, v):
+                snd_w[j - 3, i, :, pl.ds(128 * b, 128)] = v.astype(BF)
+
+        unstage(blocks, put_own, put_send)
+        if j < 3:
+            remote(snd_n.at[j], rcv_n.at[j], sn_s.at[1 + j], sn_r.at[1 + j], partner)
+        else:
+            remote(snd_w.at[j - 3], rcv_w.at[j - 3], sn_s.at[1 + j], sn_r.at[1 + j], partner)
 
     def sources_narrow():
-        wait_on(rcv_n, sn_r.at[1])
+        for j in range(3):
+            wait_on(rcv_n.at[j], sn_r.at[1 + j])
         own_n[...] = own_n[...] + rcv_n[...].astype(F32)
         copy_in(own_n, gn_out, out_s.at[3])
 
-    def chain(layer, last, first):
-        load_next = lambda f: when(layer > 0, lambda: f(layer - 1))
+    def chain(layer, last):
         b2 = lax.rem(layer, 2)
-        load_next(load_w)
-        sums = norm_backward(layer, last)
-        load_next(load_x)
+        one = layer + 1
+        two = lambda f: when(layer + 2 <= 4, lambda: f(layer + 2))
+        load_w(layer - 1)
+        output_gradient(layer, last)
+        if last:
+            send_mixed()
+            load_branch(0)
+        else:
+
+            def two_a(older):
+                add_across(older, 6)
+                add_across(older, 7)
+
+            two(two_a)
+            add_core(one, 0)
+            add_core(one, 1)
+        field_gradient(layer, last)
+        load_x(layer - 1)
+        if not last:
+            add_core(one, 2)
+            add_across(one, 0)
         halo_arrived(layer)
-
-        if last is False:
-
-            def finish_older():
-                add_across(layer + 2, 2)
-                add_across(layer + 2, 3)
-
-            when(layer + 2 <= 4, finish_older)
-            for q in range(4):
-                add_core(layer + 1, q)
         wait_on(Wl.at[0], w_s.at[b2])
-        if first is False:
-            if last is False:
-                wait_on(px.at[0], px_s)
-            acc = data_half(layer, 1 - x)
-            px[0] = acc.astype(BF)
-            remote(px.at[0], pxr.at[b2], px_s, px_r.at[layer], partner)
-            da[...] = data_half(layer, x)
-        if last is False:
-            when(layer + 2 <= 4, lambda: finish_sum(layer + 2))
-            if first:
-                for to in [across] + [(slot_z(q) * 4 + yi * 2 + ci, x) for q in range(3)]:
-                    pl.semaphore_signal(go, inc=1, device_id=to, device_id_type=MESH)
-            add_across(layer + 1, 0)
+        for j in range(4):
+            if not last:
+                wait_on(px.at[0, pl.ds(0, 256)], px_s.at[j])
+            rows = pl.ds(256 * j, 256)
+            px[0, rows, :] = data_half(layer, 1 - x, 256 * j, 256).astype(BF)
+            remote(px.at[0, rows], pxr.at[b2, rows], px_s.at[j], px_r.at[layer, j], partner)
+            if j == 1 and not last:
+                add_core(one, 3)
+                add_across(one, 1)
+        if not last:
+            two(lambda older: finish_sum(older, 0))
+        da[...] = data_half(layer, x)
+        if not last:
+            add_core(one, 4)
+            add_across(one, 2)
+            two(lambda older: finish_sum(older, 1))
             when(layer + 3 <= 4, lambda: drain_sums(layer + 3))
-        weight_gradient(layer)
-        load_next(load_h)
-        if last is False:
-            add_across(layer + 1, 1)
-        send_core(layer)
-        if last is False:
-
-            def older_out():
+        wait_on(Hl, load_s.at[1])
+        weight_gradient(layer, 0)
+        send_core(layer, (0, 1))
+        if not last:
+            add_core(one, 5)
+            add_across(one, 3)
+        weight_gradient(layer, 1)
+        send_core(layer, (2, 3))
+        load_h(layer - 1)
+        if not last:
+            add_core(one, 6)
+            add_across(one, 4)
+            add_core(one, 7)
+            add_across(one, 5)
+
+            def two_out(older):
                 when(layer + 3 <= 4, lambda: wait_assembled(32))
-                assemble(layer + 2, 32, put_rest(layer + 2))
-
-            when(layer + 2 <= 4, older_out)
-        if last:
-            branches(sums)
-        if first is False:
-            wait_on(pxr.at[0], px_r.at[layer])
-
-            def one(b, _):
-                da[rows_of(b), :] = da[rows_of(b), :] + pxr[b2, rows_of(b), :].astype(F32)
-                return 0
-
-            lax.fori_loop(0, 8, one, 0)
+                assemble(older, put_rest(older))
+
+            two(two_out)
 
     ss[...] = jnp.zeros((8, 128), F32)
-    chain(4, True, False)
-    mixers_one()
-    mixers_two()
+    chain(4, True)
+    branch(0)
 
     def middle(i, _):
         layer = 3 - i
-        chain(layer, False, False)
+        chain(layer, False)
 
         @pl.when(layer == 3)
         def _():
-            mixers_three()
+            branch(1)
+            branch(2)
             wait_on(mix_rcv, sn_r.at[0])
             copy_in(mix_rcv, mixed_out.at[:, :, other_cols], out_s.at[4])
 
         @pl.when(layer == 2)
         def _():
-            mixers_four()
+            branch(3)
+            branch(4)
+            mixers_one()
             sources_narrow()
 
         @pl.when(layer == 1)
         def _():
-            mixers_five()
+            mixers_two()
 
         return 0
 
     lax.fori_loop(0, 3, middle, 0)
-    chain(0, False, True)
+
+    output_gradient(0, False)
+    add_across(2, 6)
+    add_across(2, 7)
+    add_core(1, 0)
+    add_core(1, 1)
+    field_gradient(0, False)
+    add_core(1, 2)
+    add_across(1, 0)
+    halo_arrived(0)
+    wait_on(Hl, load_s.at[1])
+    wait_on(Wl.at[0], w_s.at[0])
+    drain_sums(3)
+    first_weight_gradient(0)
+    send_core(0, (0, 1))
+    add_core(1, 3)
+    add_across(1, 1)
+    finish_sum(2, 0)
+    add_core(1, 4)
+    add_across(1, 2)
+    first_weight_gradient(1)
+    send_core(0, (2, 3))
+    finish_sum(2, 1)
+    add_core(1, 5)
+    add_across(1, 3)
+    mixers_three()
 
     remote(ngr, ngx, ng_s, ng_r, partner)
 
     for k in range(17):
-        Wl[1, k, pl.ds(0, 12)] = (
+        Wl[1, k, pl.ds(0, 3)] = (
             jnp.dot(perm[...], Wl[0, k].reshape(512, HALF), preferred_element_type=F32)
             .astype(BF)
-            .reshape(12, 32, HALF)
+            .reshape(3, 2, 2, 32, HALF)
         )
-    add_across(1, 2)
-    pl.semaphore_wait(go, 4)
-    add_core(0, 0)
-    add_core(0, 1)
-    add_across(1, 3)
-    add_core(0, 2)
-    add_core(0, 3)
+    add_core(1, 6)
+    add_across(1, 4)
+    add_core(1, 7)
+    add_across(1, 5)
+    wait_assembled(32)
+    assemble(2, put_rest(2))
+    mixers_four()
     for part in range(4):
         acc = jnp.zeros((HALF, 384), F32)
         for k in range(17):
@@ -1680,7 +1749,7 @@
             )
             acc = acc + lax.dot_general(
                 lhs,
-                Wl[1, k, pl.ds(0, 12)].reshape(384, HALF),
+                Wl[1, k, pl.ds(0, 3)].reshape(384, HALF),
                 (((1,), (1,)), ((), ())),
                 preferred_element_type=F32,
             )
@@ -1693,6 +1762,20 @@
                     )
                     * m
                 ).reshape(128, 128)
+        if part == 0:
+            add_across(1, 6)
+            add_core(0, 0, 13)
+        if part == 1:
+            add_across(1, 7)
+            add_core(0, 1, 13)
+        if part == 2:
+            finish_sum(1, 0)
+            add_core(0, 2, 13)
+            add_across(0, 0, 13)
+        if part == 3:
+            finish_sum(1, 1)
+            add_core(0, 3, 13)
+            add_across(0, 1, 13)
 
     def put_own(i, b, v):
         lanes = pl.ds(128 * b, 128)
@@ -1702,26 +1785,34 @@
         snd_w[2, i, :, pl.ds(128 * b, 128)] = v.astype(BF)
 
     unstage(3, put_own, put_send)
-    remote(snd_w.at[2], rcv_w.at[2], sn_s.at[3], sn_r.at[3], partner)
-    add_across(0, 0)
-    finish_sum(1)
-    add_across(0, 1)
-    add_across(0, 2)
-    add_across(0, 3)
+    remote(snd_w.at[2], rcv_w.at[2], sn_s.at[6], sn_r.at[6], partner)
+    add_core(0, 4, 13)
+    add_across(0, 2, 13)
     wait_assembled(32)
-    assemble(1, 32, put_rest(1))
-    wait_on(rcv_w.at[pl.ds(0, 2)], sn_r.at[2])
-    wait_on(rcv_w.at[2], sn_r.at[3])
+    assemble(1, put_rest(1))
+    add_core(0, 5, 13)
+    add_across(0, 3, 13)
+    mixers_five()
+    add_core(0, 6, 13)
+    add_across(0, 4, 13)
+    for j in range(2):
+        wait_on(rcv_w.at[j], sn_r.at[4 + j])
+    wait_on(rcv_w.at[2], sn_r.at[6])
     for j in range(2):
         v = own_w[j] + rcv_w[j].astype(F32)
         if j == 1:
             v = v + rcv_w[2].astype(F32)
         own_w[j] = v
     copy_in(own_w, gw_out, out_s.at[5])
+    add_core(0, 7, 13)
+    add_across(0, 5, 13)
+    add_across(0, 6, 13)
+    finish_sum(0, 0, 13)
+    add_across(0, 7, 13)
+    finish_sum(0, 1, 13)
     wait_on(ngx, ng_r)
-    finish_sum(0)
     wait_assembled(32)
-    assemble(0, 24, lambda b: gf_out.at[:, pl.ds(128 * b, 128)])
+    assemble(0, lambda b: gf_out.at[:, pl.ds(128 * b, 128)], 13)
 
     fst[t] = ss[...]
 
@@ -1750,29 +1841,28 @@
     wait_on(own_w, out_s.at[5])
     wait_on(gsm.at[:, pl.ds(0, 48)], out_s.at[1])
     wait_on(gsm.at[:, pl.ds(0, 48)], out_s.at[2])
-    wait_on(px.at[0], px_s)
+    for j in range(4):
+        wait_on(px.at[0, pl.ds(0, 256)], px_s.at[j])
     wait_on(mix_own.at[1], sn_s.at[0])
-    wait_on(snd_n, sn_s.at[1])
-    wait_on(snd_w.at[pl.ds(0, 2)], sn_s.at[2])
-    wait_on(snd_w.at[2], sn_s.at[3])
+    for j in range(3):
+        wait_on(snd_n.at[0], sn_s.at[1 + j])
+        wait_on(snd_w.at[0], sn_s.at[4 + j])
     wait_on(cm, m_s.at[0])
     wait_on(ym, m_s.at[1])
     wait_on(zm, m_s.at[2])
     wait_on(fm, m_s.at[3])
     wait_on(ngr, ng_s)
     wait_on(fst.at[pl.ds(0, 15)], st_s.at[5])
-    for layer in (1, 0, 2):
-        drain_sums(layer)
+    drain_sums(2)
+    drain_sums(1)
+    drain_sums(0, 13)
 
     for layer in range(2):
-        wait_on(fin.at[0], f_s.at[layer])
+        wait_on(fin.at[0, pl.ds(0, 34 if layer else 26)], f_s.at[layer])
         halo_sent(layer)
 
-    def finish(layer, _):
-        wait_on(bst.at[layer, pl.ds(0, 15)], st_s.at[layer])
-        return 0
-
-    lax.fori_loop(0, 5, finish, 0)
+    for layer in range(5):
+        wait_on(bst.at[layer, pl.ds(0, 15), pl.ds(0, 8 if layer == 4 else 2)], st_s.at[layer])
 
 
 def run_backward(lens, norm, rs, perm, w, wmn, wmw, h, xh, y, nar, wid, cot):
@@ -1797,7 +1887,7 @@
         in_specs=[vm, vm, vm, vm, hb, vm, vm, hb, hb, hb, hb, hb, hb],
         out_specs=[hb] * 7 + [vm, vm],
         scratch_shapes=[
-            V((2, 17, 16, 32, HALF), BF),
+            V((2, 17, 4, 2, 2, 32, HALF), BF),
             V((2, ROWS, HALF), BF),
             V((ROWS, HALF), F32),
             V((2, ROWS, HALF), F32),
@@ -1806,12 +1896,12 @@
             V((ROWS, HALF), F32),
             V((2, 1168, HALF), BF),
             V((1152, HALF), BF),
-            V((3, 17, 4, 2, 2, 32, HALF), BF),
-            V((2, 17, 4, 2, 32, HALF), BF),
-            V((2, 17, 4, 32, HALF), BF),
-            V((2, 3, 17, 32, HALF), BF),
-            V((2, 17, 32, HALF), BF),
-            V((5, 17, 32, HALF), BF),
+            V((3, 34, 4, 2, 2, 16, HALF), BF),
+            V((2, 34, 4, 2, 16, HALF), BF),
+            V((3, 34, 4, 16, HALF), BF),
+            V((3, 3, 34, 16, HALF), BF),
+            V((2, 34, 16, HALF), BF),
+            V((5, 34, 16, HALF), BF),
             V((2, ROWS, HALF), BF),
             V((2, ROWS, HALF), BF),
             V((3, ROWS, 128), F32),
@@ -1832,13 +1922,13 @@
             V((4, 544, 128), F32),
             V((4, 112, 128), F32),
             V((5, 16, 8, HALF), F32),
+            V((8, HALF), F32),
             V((10, 8, HALF), F32),
             V((10, 8, HALF), F32),
             V((8, 128), F32),
             V((16, 8, 128), F32),
             dma((5,)),
             dma((2,)),
-            pltpu.SemaphoreType.REGULAR,
             dma((3,)),
             dma((5, 2)),
             dma((5, 2)),
@@ -1847,17 +1937,17 @@
             dma((5,)),
             dma((5, 4)),
             dma((5,)),
+            dma((5, 8)),
+            dma((5, 2)),
+            dma((5, 2)),
+            dma((5,)),
+            dma((5, 2)),
+            dma((4,)),
             dma((5, 4)),
-            dma((5,)),
-            dma((5,)),
-            dma((5,)),
-            dma((5,)),
-            dma,
-            dma((5,)),
             dma((4,)),
             dma((4,)),
-            dma((4,)),
-            dma((4,)),
+            dma((7,)),
+            dma((7,)),
             dma,
             dma((6,)),
             dma,

time: 524 us -> 480 us (0.916)
  Pallas kernels: 488 us -> 441 us
    pallas_call x1, Pallas kernels: 228 us -> 195 us  [run_forward(): pl.pallas_call(forward_kernel, out_shape=(S((85, 4, 2, 2, 32, HALF), BF),...]
    pallas_call x1, Pallas kernels: 260 us -> 246 us  [run_backward(): pl.pallas_call(backward_kernel, out_shape=(S((4, 128, 512), BF), S((3, 4,...]
where the time goes in v2:
time: 480 us; the launch traced here: 471 us
  Pallas kernels  441 us (92%)
  other arithmetic  20.5 us (4%)
  local copies, waits for them, and re-layouts  5.78 us (1%)
    pallas_call x1, Pallas kernels, run_backward(): pl.pallas_call(backward_kernel, out_shape=(S((4, 128, 512), BF), S((3, 4,...  246 us
    pallas_call x1, Pallas kernels, run_forward(): pl.pallas_call(forward_kernel, out_shape=(S((85, 4, 2, 2, 32, HALF), BF),...  195 us
    sub x5, other arithmetic, adamw(): return (param - rate * (update + decay * param), first_new, second_new)  18.7 us

profile of v2, /device:TPU:0, one launch (start us, length us, event | category | flops | bytes accessed | tf_op | source)
XLA Modules:
  0.0 470.5 jit_solution(7275942176923904461)
XLA Ops:
  0.7 0.7 convert_element_type.5
  1.3 0.1 broadcast_dynamic-update-slice_fusion.lens_in
  1.4 0.7 dynamic-slice_bitcast_fusion
  2.1 0.6 pad.4.norm
  2.8 0.0 copy-done.7
  2.8 194.9 %shard_map.339 = (bf16[85,4,2,2,32,256]{5,4,3,2,1,0:T(8,128)(2,1)}, bf16[3,256,256]{2,1,0:T(8,128)(2,1)}, bf16[2,512,256]{2,1,0:T(8,128)(2,1)}, bf16[5,2,1024,25...) custom-call(f32[8,256]{1,0:T(8,128)} %copy-done.7, ...), custom_call_target="tpu_custom_call" | custom-call | flops 24000000000 | bytes 60000000 | tf_op jit(solution)/shard_map/pallas_call | solution.py:953
  197.7 0.0 copy-start.6
  197.7 0.0 copy-start.5
  197.7 0.0 copy-start.3
  197.7 246.3 %shard_map.340 = (bf16[4,128,512]{2,1,0:T(8,128)(2,1)}, f32[3,4,128,256]{3,2,1,0:T(8,128)}, f32[2,4,128,384]{3,2,1,0:T(8,128)}, f32[408,512]{1,0:T(8,128)}, f32[...) custom-call(f32[8,256]{1,0:T(8,128)} %get-tuple-element.39.lens_in, ...), custom_call_target="tpu_custom_call" | custom-call | flops 46000001024 | bytes 60000000 | tf_op jit(solution)/shard_map/pallas_call | solution.py:1874
  444.1 1.2 slice.6
  446.0 0.0 copy-start
  446.0 1.1 multiply_bitcast_fusion
  447.1 0.0 copy-done.6
  447.1 1.9 multiply_subtract_fusion.4
  449.0 0.0 copy-done.5
  449.0 1.7 multiply_subtract_fusion.2
  450.7 1.8 multiply_subtract_fusion.3
  452.5 3.6 multiply_subtract_fusion.1
  456.1 9.8 %multiply_subtract_fusion = (f32[4,544,512]{2,1,0:T(8,128)}, f32[4,544,512]{2,1,0:T(8,128)}, f32[4,544,512]{2,1,0:T(8,128)}) fusion(f32[4,544,512]{2,1,0:T(8,128)} %kr.1, f32[4,544,512]{2,1,0:T(8,128)S(1)} %copy-done, f32[]{:T(128)S(6)} %min_shard_map.3, f32[4,544,512]{2,1,0:T(8,128)} %param.31, f32[4,544,512]{2,1,0:T(8,128)} %param.32), kind=kLoop, calls=%fused_computation.2 | loop fusion | flops 17825792 | bytes 31195140 | tf_op jit(solution)/shard_map/sub | solution.py:44
  465.9 0.8 copy.45
  466.7 0.0 copy-done.2
  466.7 1.1 copy.46
  467.8 1.1 copy.47
  (10 shorter events, 0.0 us)
Async XLA Ops:
  1.4 1.4 copy-start.7
  197.7 249.4 %copy-start.6 = (f32[2,10,512]{2,0,1:T(2,128)S(1)}, f32[2,10,512]{2,0,1:T(2,128)}, u32[]{:S(2)}) copy-start(f32[2,10,512]{2,0,1:T(2,128)} %param.28) | copy-start | bytes 122884
  197.7 251.3 %copy-start.5 = (f32[2,24,512]{2,1,0:T(8,128)S(1)}, f32[2,24,512]{2,1,0:T(8,128)}, u32[]{:S(2)}) copy-start(f32[2,24,512]{2,1,0:T(8,128)} %mw.1) | copy-start | bytes 294916
  197.7 254.8 %copy-start.3 = (f32[408,512]{1,0:T(8,128)S(1)}, f32[408,512]{1,0:T(8,128)}, u32[]{:S(2)}) copy-start(f32[408,512]{1,0:T(8,128)} %kf.1) | copy-start | bytes 2506756
  446.0 10.1 %copy-start = (f32[4,544,512]{2,1,0:T(8,128)S(1)}, f32[4,544,512]{2,1,0:T(8,128)}, u32[]{:S(2)}) copy-start(f32[4,544,512]{2,1,0:T(8,128)} %get-tuple-element.55) | copy-start | bytes 13369348
  456.1 9.8 %copy-start.4 = (bf16[4,128,512]{2,1,0:T(8,128)(2,1)S(1)}, bf16[4,128,512]{2,1,0:T(8,128)(2,1)}, u32[]{:S(2)}) copy-start(bf16[4,128,512]{2,1,0:T(8,128)(2,1)} %get-tuple-element.93) | copy-start | bytes 1572868
  456.1 10.6 %copy-start.2 = (f32[3,4,128,256]{3,2,1,0:T(8,128)S(1)}, f32[3,4,128,256]{3,2,1,0:T(8,128)}, u32[]{:S(2)}) copy-start(f32[3,4,128,256]{3,2,1,0:T(8,128)} %get-tuple-element.94) | copy-start | bytes 4718596
  465.9 2.0 copy-start.1
